TPU v7x, 128 devices: a whole 4x4x4 slice. The times are simulated.
128 devices in a mesh: date: 16 (over z, y_hi, core), tile: 8 (over y_lo, x).
Axes of the slice: x: 4, y: 4 (y_hi: 2, y_lo: 2; y = y_hi * 2 + y_lo), z: 4, core: 2. Of those that a mesh axis runs over, the one named last changes fastest.
Arguments:
- slc_re: float32 [64, 512, 1024], P('date', 'tile'), may hold values from -6 to 6
- slc_im: float32 [64, 512, 1024], P('date', 'tile'), may hold values from -6 to 6
- ref_dates: int32 [4], replicated, may hold values from 0 to 62, as said below
- pair_keep: int32 [4, 64], replicated, may hold values 0 or 1
- col_offsets: int32 [64], replicated, may hold values from 0 to 7
Outputs:
- coh_re: float32 [4, 64, 512, 1024], P(None, 'date', 'tile')
- coh_im: float32 [4, 64, 512, 1024], P(None, 'date', 'tile')
Inputs may be any that keep to these rules, and one draw needn't show every extreme that they name: `ref_dates`: strictly increasing; the first is 0 and the last is 62.
All inputs are finite; a program needn't handle non-finite values.
Results may differ from a plain program's by a relative error of at most 0.0003.
Values sent between devices are 32-bit elements; how exact they have to be, the bound alone decides.
A program may use at most 128 MiB of HBM per device.

v0:
```python
import jax
import jax.numpy as jnp
from jax import lax
from jax.sharding import PartitionSpec as P


def broadcast(block, axis, owner):
    block = jnp.where(lax.axis_index(axis) == owner, block, jnp.zeros_like(block))
    return lax.psum(block, axis)


def extended(cells, sides, width):
    for axis, dim in sides:
        count = lax.axis_size(axis)
        ends = count - 1
        head = lax.slice_in_dim(cells, 0, width, axis=dim)
        tail = lax.slice_in_dim(cells, cells.shape[dim] - width, cells.shape[dim], axis=dim)
        cells = jnp.concatenate(
            [
                lax.ppermute(tail, axis, [(i, (i + 1) % count) for i in range(ends)]),
                cells,
                lax.ppermute(head, axis, [((i + 1) % count, i) for i in range(ends)]),
            ],
            axis=dim,
        )
    return cells


def shift_columns(raw, offsets, cols):
    padded = jnp.pad(raw, ((0, 0), (0, 0), (0, 0), (0, 8)))

    def one_date(plane, offset):
        return lax.dynamic_slice_in_dim(plane, offset, cols, 2)

    return jax.vmap(one_date, in_axes=(1, 0), out_axes=1)(padded, offsets)


def box_window(padded, rows, cols):
    summed = padded[:, :, 0:rows]
    for k in range(1, 5):
        summed = summed + padded[:, :, k : k + rows]
    wide = jnp.pad(summed, ((0, 0), (0, 0), (0, 0), (10, 9)))
    total = wide[:, :, :, 0:cols]
    for k in range(1, 20):
        total = total + wide[:, :, :, k : k + cols]
    return total


def body(slc_re, slc_im, ref_dates, pair_keep, col_offsets):
    date_dev = slc_re.shape[0]
    rows = slc_re.shape[1]
    cols = slc_re.shape[2]
    position = lax.axis_index("date")
    base = position * date_dev
    raw = jnp.stack((slc_re, slc_im))
    own_offsets = lax.dynamic_slice_in_dim(col_offsets, base, date_dev)
    secondary = shift_columns(raw, own_offsets, cols)
    owners = ref_dates // date_dev
    slots = ref_dates % date_dev
    own_dates = base + jnp.arange(date_dev, dtype=jnp.int32)
    out_re = []
    out_im = []
    for s in range(len(ref_dates)):
        local = lax.dynamic_index_in_dim(raw, slots[s], 1, keepdims=False)
        ref = broadcast(local, "date", owners[s])
        ifg_re = ref[0][None] * secondary[0] + ref[1][None] * secondary[1]
        ifg_im = ref[1][None] * secondary[0] - ref[0][None] * secondary[1]
        pow_a = jnp.broadcast_to((ref[0] * ref[0] + ref[1] * ref[1])[None], ifg_re.shape)
        pow_b = secondary[0] * secondary[0] + secondary[1] * secondary[1]
        planes = jnp.stack((ifg_re, ifg_im, pow_a, pow_b))
        planes = extended(planes, (("tile", 2),), 2)
        boxed = box_window(planes, rows, cols)
        scale = lax.rsqrt(boxed[2] * boxed[3] + 1e-06)
        keep_row = lax.dynamic_slice_in_dim(pair_keep[s], base, date_dev)
        valid = (keep_row == 1) & (own_dates > ref_dates[s])
        out_re.append(jnp.where(valid[:, None, None], boxed[0] * scale, jnp.float32(0.0)))
        out_im.append(jnp.where(valid[:, None, None], boxed[1] * scale, jnp.float32(0.0)))
    return (jnp.stack(out_re), jnp.stack(out_im))


def solution(mesh):
    placed = (P("date", "tile", None), P("date", "tile", None), P(), P(), P())
    return jax.shard_map(
        body,
        mesh=mesh,
        in_specs=placed,
        out_specs=(P(None, "date", "tile", None), P(None, "date", "tile", None)),
        check_vma=False,
    )
```

profile of v0, /device:TPU:8, one launch (start us, length us, event | category | flops | bytes accessed | tf_op | source)
XLA Modules:
  0.0 466.8 jit_solution(1028386333256205336)
XLA Ops:
  18.8 2.9 fusion.106
  25.7 11.9 %while.1 = (s32[]{:T(128)}, f32[4,2,64,1032]{3,2,1,0:T(8,128)S(1)}, s32[4,4]{1,0:T(4,128)S(1)}, f32[4,2,64,1024]{3,2,0,1:T(8,128)}, s32[]{:T(128)}) while((s32[]{:T(128)}, f32[4,2,64,1032]{3,2,1,0:T(8,128)S(1)}, s32[4,4]{1,0:T(4,128)S(1)}, f32[4,2,64,1024]{3,2,0,1:T(8,128)}, s32[]{:T(128)}) %tuple.75), condition=%wide.while_cond, body=%wide.while_body.sunk | while | flops 2 | bytes 1049725 | solution.py:33
  29.4 2.3 bitcast_dynamic-update-slice_fusion.2
  32.3 2.3 bitcast_dynamic-update-slice_fusion.2
  37.6 132.3 %all-reduce.9.cloned.1.call-done = (f32[2,64,1024]{2,1,0:T(8,128)}, f32[2,64,1024]{2,1,0:T(8,128)}, f32[2,64,1024]{2,1,0:T(8,128)}, f32[2,64,1024]{2,1,0:T(8,128)}) async-done(((f32[2,64,1024]{2,1,0:T(8,128)}, f32[2,64,1024]{2,1,0:T(8,128)}, f32[2,64,1024]{2,1,0:T(8,128)}, f32[2,64,1024]{2,1,0:T(8,128)}), (f32[2,64,1024]{2,1,0:T(8,128)}, f32[2,64,1024]{2,1,0:T(8,128)}, f32[2,64,1024]{2,1,0:T(8,128)}, ...) | async-done | bytes 2097168 | tf_op jit(solution)/shard_map/psum | solution.py:9
  176.2 2.8 multiply_add_fusion.4
  179.7 3.4 collective-permute-start.4
  183.1 4.6 collective-permute-start.5
  192.6 7.9 %pad_maximum_fusion.11 = (f32[4,4,64,1024]{3,2,1,0:T(8,128)}, f32[4,4,64,1024]{3,2,1,0:T(8,128)}, f32[4,4,64,1024]{3,2,1,0:T(8,128)}) fusion(f32[1,4,64,1024]{3,2,1,0:T(8,128)S(1)} %get-tuple-element.60, f32[1,4,64,1024]{3,2,1,0:T(8,128)S(1)} %stack_broadcast_in_dim.8, f32[1,4,64,1024]{3,2,1,0:T(8,128)} %get-tuple-element.53, ...), kind=kLoop, calls=%fused_computation.13 | loop fusion | flops 13631488 | bytes 39845888 | tf_op jit(solution)/shard_map/stack | solution.py:70
  202.5 3.2 collective-permute-start
  205.6 5.2 %collective-permute-start.1 = (f32[4,4,2,1024]{3,2,1,0:T(2,128)S(1)}, f32[4,4,2,1024]{3,2,1,0:T(2,128)S(1)}, u32[]{:S(2)}, u32[]{:S(2)}) collective-permute-start(f32[4,4,2,1024]{3,2,1,0:T(2,128)S(1)} %get-tuple-element.39), channel_id=1, source_target_pairs={{1,0},{2,1},{3,2},{4,3},{5,4},{6,5},{7,6},{9,8},{10,9},{11,10},{12... | collective-permute-start | bytes 393224 | tf_op jit(solution)/shard_map/ppermute | solution.py:22
  214.8 6.2 %collective-permute-start.3 = (f32[4,4,2,1024]{3,2,1,0:T(2,128)}, f32[4,4,2,1024]{3,2,1,0:T(2,128)S(1)}, u32[]{:S(2)}, u32[]{:S(2)}) collective-permute-start(f32[4,4,2,1024]{3,2,1,0:T(2,128)} %get-tuple-element.43), channel_id=1, source_target_pairs={{1,0},{2,1},{3,2},{4,3},{5,4},{6,5},{7,6},{9,8},{10,9},{11,10},{12... | collective-permute-start | bytes 393224 | tf_op jit(solution)/shard_map/ppermute | solution.py:22
  221.0 51.9 %fusion.64 = f32[4,4,64,1024]{3,2,1,0:T(8,128)S(1)} fusion(f32[4,4,64,1024]{3,2,1,0:T(8,128)} %get-tuple-element.72), kind=kLoop, calls=%fused_computation.154 | loop fusion | flops 19922944 | bytes 8388608 | tf_op jit(solution)/shard_map/add | solution.py:45
  277.0 4.3 slice_add_fusion.6
  281.2 52.2 %fusion.45 = f32[4,4,64,1024]{3,2,1,0:T(8,128)S(1)} fusion(f32[4,4,64,1024]{3,2,1,0:T(8,128)} %get-tuple-element.74), kind=kLoop, calls=%fused_computation.135 | loop fusion | flops 19922944 | bytes 8388608 | tf_op jit(solution)/shard_map/add | solution.py:45
  336.7 6.0 %collective-permute-start.7 = (f32[4,4,2,1024]{3,2,1,0:T(2,128)S(1)}, f32[4,4,2,1024]{3,2,1,0:T(2,128)S(1)}, u32[]{:S(2)}, u32[]{:S(2)}) collective-permute-start(f32[4,4,2,1024]{3,2,1,0:T(2,128)S(1)} %get-tuple-element.51), channel_id=1, source_target_pairs={{1,0},{2,1},{3,2},{4,3},{5,4},{6,5},{7,6},{9,8},{10,9},{11,10},{12... | collective-permute-start | bytes 393224 | tf_op jit(solution)/shard_map/ppermute | solution.py:22
  342.8 7.2 %fusion.4 = (f32[4,4,66,1024]{3,2,1,0:T(8,128)}, f32[4,4,66,1024]{3,2,1,0:T(8,128)}) fusion(f32[1,4,64,1024]{3,2,1,0:T(8,128)S(1)} %get-tuple-element.60, f32[1,4,64,1024]{3,2,1,0:T(8,128)} %copy-done.2, f32[1,4,64,1024]{3,2,1,0:T(8,128)} %get-tuple-element.53, f32[1,4,64,1024]{3,2,1,0:T(8,128)} %get-tuple-element.52, ...), kind=kLoop, calls=%fused_computation.18 | loop fusion | flops 8650752 | bytes 13107200 | tf_op jit(solution)/shard_map/concatenate | solution.py:18
  351.9 4.1 fusion.7
  356.0 19.4 %slice_add_fusion.9 = (f32[4,4,64,1024]{3,2,1,0:T(8,128)}, f32[4,4,64,1024]{3,2,1,0:T(8,128)}) fusion(f32[4,4,66,1024]{3,2,1,0:T(8,128)} %get-tuple-element.37, f32[4,4,66,1024]{3,2,1,0:T(8,128)} %get-tuple-element.36, f32[1,4,64,1024]{3,2,1,0:T(8,128)S(1)} %get-tuple-element.60, f32[1,4,64,1024]{3,2,1,0:T(8,128)} %copy-done.2, ...), kind=kLoop, calls=%fused_computation.186 | loop fusion | flops 14680064 | bytes 49283072 | tf_op jit(solution)/shard_map/add | solution.py:41
  375.4 53.3 %fusion.26 = f32[4,4,64,1024]{3,2,1,0:T(8,128)} fusion(f32[4,4,64,1024]{3,2,1,0:T(8,128)} %get-tuple-element.69), kind=kLoop, calls=%fused_computation.116 | loop fusion | flops 19922944 | bytes 8388608 | tf_op jit(solution)/shard_map/add | solution.py:45
  428.7 22.1 %fusion.83 = f32[4,4,64,1024]{3,2,1,0:T(8,128)} fusion(f32[4,4,64,1024]{3,2,1,0:T(8,128)S(1)} %copy-done), kind=kLoop, calls=%fused_computation.173 | loop fusion | flops 19922944 | bytes 8388608 | tf_op jit(solution)/shard_map/add | solution.py:45
  450.8 2.8 fusion.91
  455.3 2.3 pad_maximum_fusion.13
  457.6 2.3 pad_maximum_fusion.12
  (104 shorter events, 41.2 us)
Async XLA Ops:
  7.2 14.6 %copy-start.20 = (s32[4]{0:T(128)S(1)}, s32[4]{0:T(128)}, u32[]{:S(2)}) copy-start(s32[4]{0:T(128)} %param.7) | copy-start | bytes 52
  7.2 18.1 %copy-start.12 = (f32[4,64,1024]{2,1,0:T(8,128)S(1)}, f32[4,64,1024]{2,1,0:T(8,128)}, u32[]{:S(2)}) copy-start(f32[4,64,1024]{2,1,0:T(8,128)} %param.6) | copy-start | bytes 3145732
  7.2 18.1 %copy-start.13 = (f32[4,64,1024]{2,1,0:T(8,128)S(1)}, f32[4,64,1024]{2,1,0:T(8,128)}, u32[]{:S(2)}) copy-start(f32[4,64,1024]{2,1,0:T(8,128)} %param.5) | copy-start | bytes 3145732
  7.2 15.2 %copy-start.22 = (s32[64]{0:T(128)S(1)}, s32[64]{0:T(128)}, u32[]{:S(2)}) copy-start(s32[64]{0:T(128)} %param.9) | copy-start | bytes 772
  7.2 15.4 %copy-start.21 = (s32[4,64]{1,0:T(4,128)S(1)}, s32[4,64]{1,0:T(4,128)}, u32[]{:S(2)}) copy-start(s32[4,64]{1,0:T(4,128)} %param.8) | copy-start | bytes 3076
  7.2 162.7 %all-reduce.9.cloned.1.call-start = ((), (), s32[]{:S(2)}) async-start(), calls=%async_computation | async-start | bytes 4194304 | tf_op jit(solution)/shard_map/psum | solution.py:9
  169.9 5.5 %copy-start.19 = (f32[2,64,1024]{2,1,0:T(8,128)S(1)}, f32[2,64,1024]{2,1,0:T(8,128)}, u32[]{:S(2)}) copy-start(f32[2,64,1024]{2,1,0:T(8,128)} %get-tuple-element.24) | copy-start | bytes 1572868
  169.9 5.5 %copy-start.18 = (f32[2,64,1024]{2,1,0:T(8,128)S(1)}, f32[2,64,1024]{2,1,0:T(8,128)}, u32[]{:S(2)}) copy-start(f32[2,64,1024]{2,1,0:T(8,128)} %get-tuple-element.25) | copy-start | bytes 1572868
  169.9 5.6 %copy-start.11 = (f32[4,2,64,1024]{3,2,0,1:T(8,128)S(1)}, f32[4,2,64,1024]{3,2,0,1:T(8,128)}, u32[]{:S(2)}) copy-start(f32[4,2,64,1024]{3,2,0,1:T(8,128)} %get-tuple-element.9) | copy-start | bytes 6291460
  176.2 14.0 %copy-start.8 = (f32[1,4,64,1024]{3,2,1,0:T(8,128)}, f32[1,4,64,1024]{3,2,1,0:T(8,128)S(1)}, u32[]{:S(2)}) copy-start(f32[1,4,64,1024]{3,2,1,0:T(8,128)S(1)} %get-tuple-element.56) | copy-start | bytes 3145732
  176.2 14.0 %copy-start.9 = (f32[1,4,64,1024]{3,2,1,0:T(8,128)}, f32[1,4,64,1024]{3,2,1,0:T(8,128)S(1)}, u32[]{:S(2)}) copy-start(f32[1,4,64,1024]{3,2,1,0:T(8,128)S(1)} %get-tuple-element.57) | copy-start | bytes 3145732
  179.1 11.0 %copy-start.10 = (f32[1,4,64,1024]{3,2,1,0:T(8,128)}, f32[1,4,64,1024]{3,2,1,0:T(8,128)S(1)}, u32[]{:S(2)}) copy-start(f32[1,4,64,1024]{3,2,1,0:T(8,128)S(1)} %stack_broadcast_in_dim.10) | copy-start | bytes 3145732
  179.7 9.0 %collective-permute-start.4 = (f32[4,4,2,1024]{3,2,1,0:T(2,128)S(1)}, f32[4,4,2,1024]{3,2,1,0:T(2,128)S(1)}, u32[]{:S(2)}, u32[]{:S(2)}) collective-permute-start(f32[4,4,2,1024]{3,2,1,0:T(2,128)S(1)} %get-tuple-element.46), channel_id=1, source_target_pairs={{0,1},{1,2},{2,3},{3,4},{4,5},{5,6},{6,7},{8,9},{9,10},{10,11},{11... | collective-permute-start | bytes 393224 | tf_op jit(solution)/shard_map/ppermute | solution.py:20
  183.1 7.1 %collective-permute-start.5 = (f32[4,4,2,1024]{3,2,1,0:T(2,128)S(1)}, f32[4,4,2,1024]{3,2,1,0:T(2,128)S(1)}, u32[]{:S(2)}, u32[]{:S(2)}) collective-permute-start(f32[4,4,2,1024]{3,2,1,0:T(2,128)S(1)} %get-tuple-element.47), channel_id=1, source_target_pairs={{1,0},{2,1},{3,2},{4,3},{5,4},{6,5},{7,6},{9,8},{10,9},{11,10},{12... | collective-permute-start | bytes 393224 | tf_op jit(solution)/shard_map/ppermute | solution.py:22
  191.4 9.1 %copy-start.2 = (f32[1,4,64,1024]{3,2,1,0:T(8,128)}, f32[1,4,64,1024]{3,2,1,0:T(8,128)S(1)}, u32[]{:S(2)}) copy-start(f32[1,4,64,1024]{3,2,1,0:T(8,128)S(1)} %stack_broadcast_in_dim.8) | copy-start | bytes 3145732
  202.5 140.3 %collective-permute-start = (f32[4,4,2,1024]{3,2,1,0:T(2,128)}, f32[4,4,2,1024]{3,2,1,0:T(2,128)S(1)}, u32[]{:S(2)}, u32[]{:S(2)}) collective-permute-start(f32[4,4,2,1024]{3,2,1,0:T(2,128)} %get-tuple-element.38), channel_id=1, source_target_pairs={{0,1},{1,2},{2,3},{3,4},{4,5},{5,6},{6,7},{8,9},{9,10},{10,11},{11... | collective-permute-start | bytes 393224 | tf_op jit(solution)/shard_map/ppermute | solution.py:20
  205.6 137.1 %collective-permute-start.1 = (f32[4,4,2,1024]{3,2,1,0:T(2,128)S(1)}, f32[4,4,2,1024]{3,2,1,0:T(2,128)S(1)}, u32[]{:S(2)}, u32[]{:S(2)}) collective-permute-start(f32[4,4,2,1024]{3,2,1,0:T(2,128)S(1)} %get-tuple-element.39), channel_id=1, source_target_pairs={{1,0},{2,1},{3,2},{4,3},{5,4},{6,5},{7,6},{9,8},{10,9},{11,10},{12... | collective-permute-start | bytes 393224 | tf_op jit(solution)/shard_map/ppermute | solution.py:22
  212.9 61.9 %collective-permute-start.2 = (f32[4,4,2,1024]{3,2,1,0:T(2,128)}, f32[4,4,2,1024]{3,2,1,0:T(2,128)S(1)}, u32[]{:S(2)}, u32[]{:S(2)}) collective-permute-start(f32[4,4,2,1024]{3,2,1,0:T(2,128)} %get-tuple-element.42), channel_id=1, source_target_pairs={{0,1},{1,2},{2,3},{3,4},{4,5},{5,6},{6,7},{8,9},{9,10},{10,11},{11... | collective-permute-start | bytes 393224 | tf_op jit(solution)/shard_map/ppermute | solution.py:20
  214.8 60.0 %collective-permute-start.3 = (f32[4,4,2,1024]{3,2,1,0:T(2,128)}, f32[4,4,2,1024]{3,2,1,0:T(2,128)S(1)}, u32[]{:S(2)}, u32[]{:S(2)}) collective-permute-start(f32[4,4,2,1024]{3,2,1,0:T(2,128)} %get-tuple-element.43), channel_id=1, source_target_pairs={{1,0},{2,1},{3,2},{4,3},{5,4},{6,5},{7,6},{9,8},{10,9},{11,10},{12... | collective-permute-start | bytes 393224 | tf_op jit(solution)/shard_map/ppermute | solution.py:22
  277.0 4.3 copy-start.3
  334.8 17.1 %collective-permute-start.6 = (f32[4,4,2,1024]{3,2,1,0:T(2,128)S(1)}, f32[4,4,2,1024]{3,2,1,0:T(2,128)S(1)}, u32[]{:S(2)}, u32[]{:S(2)}) collective-permute-start(f32[4,4,2,1024]{3,2,1,0:T(2,128)S(1)} %get-tuple-element.50), channel_id=1, source_target_pairs={{0,1},{1,2},{2,3},{3,4},{4,5},{5,6},{6,7},{8,9},{9,10},{10,11},{11... | collective-permute-start | bytes 393224 | tf_op jit(solution)/shard_map/ppermute | solution.py:20
  336.7 15.2 %collective-permute-start.7 = (f32[4,4,2,1024]{3,2,1,0:T(2,128)S(1)}, f32[4,4,2,1024]{3,2,1,0:T(2,128)S(1)}, u32[]{:S(2)}, u32[]{:S(2)}) collective-permute-start(f32[4,4,2,1024]{3,2,1,0:T(2,128)S(1)} %get-tuple-element.51), channel_id=1, source_target_pairs={{1,0},{2,1},{3,2},{4,3},{5,4},{6,5},{7,6},{9,8},{10,9},{11,10},{12... | collective-permute-start | bytes 393224 | tf_op jit(solution)/shard_map/ppermute | solution.py:22
  375.4 53.3 %copy-start = (f32[4,4,64,1024]{3,2,1,0:T(8,128)S(1)}, f32[4,4,64,1024]{3,2,1,0:T(8,128)}, u32[]{:S(2)}) copy-start(f32[4,4,64,1024]{3,2,1,0:T(8,128)} %get-tuple-element.70) | copy-start | bytes 12582916
  450.8 3.4 copy-start.1
  (8 other events, 16.0 us)
Sparse Core Ops, SparseCore 0:
  21.9 147.9 all-reduce.8
where the time goes:
time: 468 us; the launch traced here: 467 us
  other arithmetic  250 us (53%)
  waiting for transfers between devices  135 us (29%)
  starting transfers between devices  32.5 us (7%)
  between operations  24.6 us (5%)
  local copies, waits for them, and re-layouts  24.5 us (5%)
    add x4, other arithmetic, box_window(): total = total + wide[:, :, :, k:k + cols]  179 us
    psum x1, waiting for transfers between devices, broadcast(): return lax.psum(block, axis)  132 us
    add x2, other arithmetic, box_window(): summed = summed + padded[:, :, k:k + rows]  23.6 us
    ppermute x4, starting transfers between devices, extended(): lax.ppermute(head, axis, [((i + 1) % count, i) for i in range(ends)])  22 us
    concatenate x4, other arithmetic, extended(): jnp.concatenate([lax.ppermute(tail, axis, [(i, (i + 1) % count) for i in...  13.7 us
    gather x12, local copies, waits for them, and re-layouts  11.8 us
    ppermute x4, starting transfers between devices, extended(): lax.ppermute(tail, axis, [(i, (i + 1) % count) for i in range(ends)])  10.4 us
  transfers between devices with their start and end apart: 9, of which 3 were waited for; matrix products, arithmetic and copies ran while one was open for 30% of the time, Pallas kernels for 0%

commit v1 on v0

v1 whole, which is shorter than its diff:
```python
import jax
import jax.numpy as jnp
import numpy as np
from jax import lax
from jax.experimental import pallas as pl
from jax.experimental.pallas import tpu as pltpu
from jax.sharding import PartitionSpec as P

MESH = pl.DeviceIdType.MESH
DATE_DEV = 4
ROWS = 64
COLS = 1024
BLOCKS = COLS // 128
REFS = 3
VMEM_LIMIT = 56 * 2**20


def band_matrix():
    k = np.arange(128)[:, None]
    c = np.arange(128)[None, :]
    middle = (k >= c - 10) & (k <= c + 9)
    edge = ((c < 10) & (k >= 118 + c)) | ((c >= 119) & (k <= c - 119))
    half = np.concatenate([middle, edge], axis=1)
    return jnp.asarray(np.concatenate([half, half], axis=0), jnp.bfloat16)


def device(z, y, core):
    return {"date": (z * 2 + y) * 2 + core}


def spread_kernel(owners, dates_ref, re_ref, im_ref, refs, ref_edges, left, right, own_edges, twin, twin_edges, send, recv, edge_send, edge_recv):
    me = lax.axis_index("date")
    tile = lax.axis_index("tile")
    z, y, core = me // 4, (me // 2) % 2, me % 2
    tiles = lax.axis_size("tile")
    next_tile = {"tile": lax.rem(tile + 1, tiles)}
    last_tile = {"tile": lax.rem(tile + tiles - 1, tiles)}
    sibling = device(z, y, 1 - core)

    def owner(s):
        z0, y0 = owners[0]
        for k in range(1, REFS):
            z0 = jnp.where(s == k, owners[k][0], z0)
            y0 = jnp.where(s == k, owners[k][1], y0)
        return z0, y0

    barrier = pltpu.get_barrier_semaphore()

    def greet(target):
        pl.semaphore_signal(barrier, inc=1, device_id=target, device_id_type=MESH)

    greet(next_tile)
    greet(last_tile)
    greet(sibling)

    @pl.loop(1, 8)
    def _(k):
        greet({"date": lax.rem(me + 2 * k, 16)})

    for j in range(DATE_DEV):
        own_edges[j, 0:2] = re_ref[j, 0:2]
        own_edges[j, 2:4] = re_ref[j, ROWS - 2 : ROWS]
        own_edges[j, 4:6] = im_ref[j, 0:2]
        own_edges[j, 6:8] = im_ref[j, ROWS - 2 : ROWS]

    @pl.loop(0, REFS)
    def _(s):
        z0, y0 = owner(s)

        @pl.when((z == z0) & (y == y0))
        def _():
            slot = lax.rem(dates_ref[s], DATE_DEV)
            refs[s, 0] = re_ref[slot]
            refs[s, 1] = im_ref[slot]

    pl.semaphore_wait(barrier, 10)

    def edge_copy(k, source, target, to):
        return pltpu.make_async_remote_copy(
            src_ref=source, dst_ref=target, send_sem=edge_send.at[k], recv_sem=edge_recv.at[k], device_id=to, device_id_type=MESH
        )

    to_right = edge_copy(0, own_edges, left, next_tile)
    to_left = edge_copy(1, own_edges, right, last_tile)

    def copy(s, source, target, out, slot, to):
        return pltpu.make_async_remote_copy(
            src_ref=source, dst_ref=target, send_sem=send.at[s, out], recv_sem=recv.at[s, slot], device_id=to, device_id_type=MESH
        )

    def quarter(s, ring, plane):
        return refs.at[s, :, pl.ds(pl.multiple_of(plane * 32 + ring * 16, 16), 16), :]

    def whole(s):
        return copy(s, refs.at[s], twin.at[s], 7, 4, sibling)

    def edges_whole(s):
        return copy(s, ref_edges.at[s], twin_edges.at[s], 8, 6, sibling)

    def along(s, level):
        return copy(s, quarter(s, y, core), quarter(s, y, core), level, 0, device(level, y, core))

    def across(s, ring, slot):
        return copy(s, quarter(s, ring, core), quarter(s, ring, core), 4 if slot else 0, slot, device(z, 1 - y, core))

    def inward(s, ring, slot):
        return copy(s, quarter(s, ring, core), quarter(s, ring, core), 5 + slot, 2 + slot, sibling)

    def edges_out(s, k):
        return copy(s, ref_edges.at[s], ref_edges.at[s], 8 + k, 5, {"date": lax.rem(me + 2 * k, 16)})

    def roles(s):
        z0, y0 = owner(s)
        source = (z == z0) & (y == y0)
        relay = (z == z0) & (y != y0)
        beyond = z > z0
        return z0, y0, source, relay, beyond

    def to_levels(s, act):
        z0, _ = owner(s)

        @pl.loop(1, 4)
        def _(level):
            @pl.when(level > z0)
            def _():
                act(along(s, level))

    def to_all(s, act):
        z0, _ = owner(s)

        @pl.loop(1, 8)
        def _(k):
            @pl.when(lax.rem(me + 2 * k, 16) // 4 >= z0)
            def _():
                act(edges_out(s, k))

    @pl.loop(0, REFS)
    def _(s):
        @pl.when(roles(s)[2])
        def _():
            whole(s).start()

    to_right.start()
    to_left.start()

    @pl.loop(0, REFS)
    def _(s):
        z0, y0, source, relay, beyond = roles(s)

        @pl.when(source)
        def _():
            whole(s).wait()
            mine = lax.rem(dates_ref[s] // DATE_DEV, 2) == core
            refs[s] = jnp.where(mine, refs[s], twin[s])
            across(s, 1 - y, 0).start()
            to_levels(s, lambda c: c.start())
            across(s, y, 1).start()

    to_right.wait_recv()
    to_left.wait_recv()

    @pl.loop(0, REFS)
    def _(s):
        @pl.when(roles(s)[2])
        def _():
            slot = lax.rem(dates_ref[s], DATE_DEV)
            ref_edges[s, 0:2] = left[slot, 2:4]
            ref_edges[s, 2:4] = right[slot, 0:2]
            ref_edges[s, 4:6] = left[slot, 6:8]
            ref_edges[s, 6:8] = right[slot, 4:6]
            edges_whole(s).start()

    @pl.loop(0, REFS)
    def _(s):
        @pl.when(roles(s)[2])
        def _():
            edges_whole(s).wait()
            mine = lax.rem(dates_ref[s] // DATE_DEV, 2) == core
            ref_edges[s] = jnp.where(mine, ref_edges[s], twin_edges[s])
            to_all(s, lambda c: c.start())

    @pl.loop(0, REFS)
    def _(s):
        z0, y0, source, relay, beyond = roles(s)

        @pl.when(relay | beyond)
        def _():
            copy(s, quarter(s, y, core), quarter(s, y, core), 0, 0, sibling).wait_recv()

            @pl.when(relay)
            def _():
                to_levels(s, lambda c: c.start())

            @pl.when(beyond)
            def _():
                across(s, y, 1).start()

            inward(s, y, 0).start()

    @pl.loop(0, REFS)
    def _(s):
        z0, y0, source, relay, beyond = roles(s)

        @pl.when(relay | beyond)
        def _():
            copy(s, quarter(s, 1 - y, core), quarter(s, 1 - y, core), 0, 1, sibling).wait_recv()
            inward(s, 1 - y, 1).start()

    @pl.loop(0, REFS)
    def _(s):
        z0, y0, source, relay, beyond = roles(s)

        @pl.when(relay | beyond)
        def _():
            edges_out(s, 1).wait_recv()
            copy(s, quarter(s, y, 1 - core), quarter(s, y, 1 - core), 0, 2, sibling).wait_recv()
            copy(s, quarter(s, 1 - y, 1 - core), quarter(s, 1 - y, 1 - core), 0, 3, sibling).wait_recv()
            inward(s, y, 0).wait_send()
            inward(s, 1 - y, 1).wait_send()

        @pl.when(source | relay)
        def _():
            to_levels(s, lambda c: c.wait_send())

        @pl.when(source)
        def _():
            across(s, 1 - y, 0).wait_send()
            to_all(s, lambda c: c.wait_send())

        @pl.when(source | beyond)
        def _():
            across(s, y, 1).wait_send()

    to_right.wait_send()
    to_left.wait_send()


def spread(first, second, number):
    owners = [(chip // 2, chip % 2) for chip in (0, first, second)]

    def kernel(*refs):
        spread_kernel(owners, *refs)

    vmem = pl.BlockSpec(memory_space=pltpu.VMEM)

    def call(dates, slc_re, slc_im):
        return pl.pallas_call(
            kernel,
            out_shape=(
                jax.ShapeDtypeStruct((REFS, 2, ROWS, COLS), jnp.float32),
                jax.ShapeDtypeStruct((REFS, 8, COLS), jnp.float32),
                jax.ShapeDtypeStruct((DATE_DEV, 8, COLS), jnp.float32),
                jax.ShapeDtypeStruct((DATE_DEV, 8, COLS), jnp.float32),
            ),
            in_specs=[pl.BlockSpec(memory_space=pltpu.SMEM), vmem, vmem],
            out_specs=(vmem, vmem, vmem, vmem),
            scratch_shapes=[
                pltpu.VMEM((DATE_DEV, 8, COLS), jnp.float32),
                pltpu.VMEM((REFS, 2, ROWS, COLS), jnp.float32),
                pltpu.VMEM((REFS, 8, COLS), jnp.float32),
                pltpu.SemaphoreType.DMA((REFS, 16)),
                pltpu.SemaphoreType.DMA((REFS, 7)),
                pltpu.SemaphoreType.DMA((2,)),
                pltpu.SemaphoreType.DMA((2,)),
            ],
            compiler_params=pltpu.CompilerParams(collective_id=number, has_side_effects=True, vmem_limit_bytes=VMEM_LIMIT),
            name=f"spread_{first}_{second}",
        )(dates, slc_re, slc_im)

    return call


def pick_kernel(dates_ref, pick_ref):
    first = dates_ref[1] // (2 * DATE_DEV)
    second = dates_ref[2] // (2 * DATE_DEV)
    pick_ref[0] = (first * (17 - first)) // 2 + (second - first)


def compute_kernel(
    dates_ref, keep_ref, offsets_ref, re_ref, im_ref, left, right, refs, ref_edges, band, out_re, out_im, a_ext, b_ext, prod, wide, pow_a, pow_b
):
    j = pl.program_id(0)
    s = pl.program_id(1)
    me = lax.axis_index("date")
    tile = lax.axis_index("tile")
    date = me * DATE_DEV + j
    has_top = (tile > 0).astype(jnp.float32)
    has_bottom = (tile < lax.axis_size("tile") - 1).astype(jnp.float32)
    valid = (keep_ref[s, date] == 1) & (date > dates_ref[s])

    def lay(ext, plane, rows, top, bottom):
        top = top * has_top
        bottom = bottom * has_bottom
        for g in range(BLOCKS):
            cut = slice(128 * g, 128 * g + 128)
            ext[plane, g, 0:2] = top[:, cut]
            ext[plane, g, 2 : ROWS + 2] = rows[:, cut]
            ext[plane, g, ROWS + 2 : ROWS + 4] = bottom[:, cut]

    def widen(count):
        for g in range(BLOCKS):
            for p in range(count):
                total = prod[p, g, 0:ROWS]
                for k in range(1, 5):
                    total = total + prod[p, g, k : k + ROWS]
                high = total.astype(jnp.bfloat16)
                low = (total - high.astype(jnp.float32)).astype(jnp.bfloat16)
                wide[g, p * ROWS : (p + 1) * ROWS, 0:128] = high
                wide[g, p * ROWS : (p + 1) * ROWS, 128:256] = low

    def columns(count):
        rows = count * ROWS
        lhs = wide[:, 0:rows, :].reshape(BLOCKS * rows, 256)
        return jnp.dot(lhs, band[...], preferred_element_type=jnp.float32).reshape(BLOCKS, rows, 256)

    lane = lax.broadcasted_iota(jnp.int32, (ROWS, 128), 1)

    def joined(sums, g, p):
        rows = slice(p * ROWS, (p + 1) * ROWS)
        zero = jnp.zeros((ROWS, 128), jnp.float32)
        before = sums[g - 1, rows, 128:256] if g > 0 else zero
        after = sums[g + 1, rows, 128:256] if g < BLOCKS - 1 else zero
        return sums[g, rows, 0:128] + jnp.where(lane < 64, before, after)

    def power(ext, out):
        for g in range(BLOCKS):
            prod[0, g, 0:72] = ext[0, g] * ext[0, g] + ext[1, g] * ext[1, g]
        widen(1)
        sums = columns(1)
        for g in range(BLOCKS):
            out[g] = joined(sums, g, 0)

    @pl.when((j == 0) & (s < REFS))
    def _():
        at = jnp.minimum(s, REFS - 1)
        edges = ref_edges[at]
        lay(a_ext.at[s], 0, refs[at, 0], edges[0:2], edges[2:4])
        lay(a_ext.at[s], 1, refs[at, 1], edges[4:6], edges[6:8])
        power(a_ext.at[s], pow_a.at[s])

    @pl.when((s == REFS) & valid)
    def _():
        edges_left = left[DATE_DEV - 2]
        edges_right = right[DATE_DEV - 2]
        lay(a_ext.at[s], 0, re_ref[DATE_DEV - 2], edges_left[2:4], edges_right[0:2])
        lay(a_ext.at[s], 1, im_ref[DATE_DEV - 2], edges_left[6:8], edges_right[4:6])
        power(a_ext.at[s], pow_a.at[s])

    @pl.when(s == 0)
    def _():
        offset = offsets_ref[date]
        turn = lax.rem(COLS - offset, COLS)

        def shifted(x):
            column = lax.broadcasted_iota(jnp.int32, x.shape, 1)
            return jnp.where(column < COLS - offset, pltpu.roll(x, turn, 1), 0.0)

        edges_left = shifted(left[j])
        edges_right = shifted(right[j])
        lay(b_ext, 0, shifted(re_ref[j]), edges_left[2:4], edges_right[0:2])
        lay(b_ext, 1, shifted(im_ref[j]), edges_left[6:8], edges_right[4:6])
        power(b_ext, pow_b)

    @pl.when(valid)
    def _():
        for g in range(BLOCKS):
            a_re, a_im = a_ext[s, 0, g], a_ext[s, 1, g]
            b_re, b_im = b_ext[0, g], b_ext[1, g]
            prod[0, g] = a_re * b_re + a_im * b_im
            prod[1, g] = a_im * b_re - a_re * b_im
        widen(2)
        sums = columns(2)
        for g in range(BLOCKS):
            scale = lax.rsqrt(pow_a[s, g] * pow_b[g] + 1e-06)
            out_re[0, 0, :, 128 * g : 128 * g + 128] = joined(sums, g, 0) * scale
            out_im[0, 0, :, 128 * g : 128 * g + 128] = joined(sums, g, 1) * scale

    @pl.when(jnp.logical_not(valid))
    def _():
        out_re[...] = jnp.zeros_like(out_re)
        out_im[...] = jnp.zeros_like(out_im)


def compute(dates, keep, offsets, slc_re, slc_im, left, right, refs, ref_edges):
    steps = REFS + 1
    smem = pl.BlockSpec(memory_space=pltpu.SMEM)
    vmem = pl.BlockSpec(memory_space=pltpu.VMEM)
    shape = jax.ShapeDtypeStruct((steps, DATE_DEV, ROWS, COLS), jnp.float32)
    out = pl.BlockSpec((1, 1, ROWS, COLS), lambda j, s: (s, j, 0, 0))
    return pl.pallas_call(
        compute_kernel,
        grid=(DATE_DEV, steps),
        out_shape=(shape, shape),
        in_specs=[smem, smem, smem] + [vmem] * 7,
        out_specs=(out, out),
        scratch_shapes=[
            pltpu.VMEM((steps, 2, BLOCKS, 72, 128), jnp.float32),
            pltpu.VMEM((2, BLOCKS, 72, 128), jnp.float32),
            pltpu.VMEM((2, BLOCKS, 72, 128), jnp.float32),
            pltpu.VMEM((BLOCKS, 2 * ROWS, 256), jnp.bfloat16),
            pltpu.VMEM((steps, BLOCKS, ROWS, 128), jnp.float32),
            pltpu.VMEM((BLOCKS, ROWS, 128), jnp.float32),
        ],
        compiler_params=pltpu.CompilerParams(vmem_limit_bytes=VMEM_LIMIT),
        name="coherence",
    )(dates, keep, offsets, slc_re, slc_im, left, right, refs, ref_edges, band_matrix())


def body(slc_re, slc_im, ref_dates, pair_keep, col_offsets):
    pick = pl.pallas_call(
        pick_kernel,
        out_shape=jax.ShapeDtypeStruct((1,), jnp.int32),
        in_specs=[pl.BlockSpec(memory_space=pltpu.SMEM)],
        out_specs=pl.BlockSpec(memory_space=pltpu.SMEM),
        name="pick",
    )(ref_dates)[0]
    pairs = [(first, second) for first in range(8) for second in range(first, 8)]
    branches = [spread(first, second, number) for number, (first, second) in enumerate(pairs)]
    refs, ref_edges, left, right = lax.switch(pick, branches, ref_dates, slc_re, slc_im)
    return compute(ref_dates, pair_keep, col_offsets, slc_re, slc_im, left, right, refs, ref_edges)


def solution(mesh):
    placed = (P("date", "tile", None), P("date", "tile", None), P(), P(), P())
    return jax.shard_map(
        body,
        mesh=mesh,
        in_specs=placed,
        out_specs=(P(None, "date", "tile", None), P(None, "date", "tile", None)),
        check_vma=False,
    )
```

time: 468 us -> 51.9 us (0.11)
  the two profiles are of different devices: /device:TPU:8 before, /device:TPU:97 now
where the time goes in v1:
time: 51.9 us; the launch traced here: 51.7 us
  Pallas kernels  50.2 us (97%)
  between operations  1.29 us (2%)
    pallas_call x1, Pallas kernels, call(): pl.pallas_call(kernel, out_shape=(jax.ShapeDtypeStruct((REFS, 2, ROWS, CO...  36.4 us
    pallas_call x1, Pallas kernels, compute(): pl.pallas_call(compute_kernel, grid=(DATE_DEV, steps), out_shape=(shape,...  12.6 us
    pallas_call x1, Pallas kernels, body(): pl.pallas_call(pick_kernel, out_shape=jax.ShapeDtypeStruct((1,), jnp.int3...  1.2 us

profile of v1, /device:TPU:97, one launch (start us, length us, event | category | flops | bytes accessed | tf_op | source)
XLA Modules:
  0.0 51.7 jit_solution(864869054520090001)
XLA Ops:
  0.6 1.2 %pick.1 = s32[1]{0:T(128)} custom-call(s32[4]{0:T(128)} %dates_ref.3), custom_call_target="tpu_custom_call" | custom-call | tf_op jit(solution)/shard_map/pick/pallas_call | solution.py:410
  2.5 36.7 %conditional.1 = ((f32[3,2,64,1024]{3,2,1,0:T(8,128)S(1)}, f32[3,8,1024]{2,1,0:T(8,128)S(1)}, f32[4,8,1024]{2,1,0:T(8,128)S(1)}, f32[4,8,1024]{2,1,0:T(8,128)S(1)})) conditional(s32[]{:T(128)} %bitcast, (s32[4]{0:T(128)}, f32[4,64,1024]{2,1,0:T(8,128)}, f32[4,64,1024]{2,1,0:T(8,128)}) %tuple.115, (s32[4]{0:T(128)}, ...), branch_computations={%region_0.0_spmd, %region_1.0_spmd, %region_2.0_spmd, %region_3.0_... | conditional | bytes 8 | solution.py:419
  2.7 36.4 %spread_4_6.1 = (f32[3,2,64,1024]{3,2,1,0:T(8,128)S(1)}, f32[3,8,1024]{2,1,0:T(8,128)S(1)}, f32[4,8,1024]{2,1,0:T(8,128)S(1)}, f32[4,8,1024]{2,1,0:T(8,128)S(1)}) custom-call(s32[4]{0:T(128)} %get-tuple-element.300.refs_0_, f32[4,64,1024]{2,1,0:T(8,128)} %get-tuple-element.301.refs_1_, f32[4,64,1024]{2,1,0:T(8,128)} %get-tuple-element.302.refs_2_), custom_call_target="tpu_custom_call" | custom-call | tf_op jit(solution)/shard_map/cond/branch_28_fun/spread_4_6/pallas_call | solution.py:247
  39.2 12.6 %coherence.1 = (f32[4,4,64,1024]{3,2,1,0:T(8,128)}, f32[4,4,64,1024]{3,2,1,0:T(8,128)}) custom-call(s32[4]{0:T(128)} %dates_ref.3, s32[4,64]{1,0:T(4,128)} %keep_ref.1, s32[64]{0:T(128)} %offsets_ref.1, f32[4,64,1024]{2,1,0:T(8,128)} %re_ref.1, f32[4,64,1024]{2,1,0:T(8,128)} %im_ref.1, f32[4,8,1024]{2,1,0:T(8,128)S(1)} %get-tuple-element.330.left, ...), custom_call_target="tpu_custom_call" | custom-call | tf_op jit(solution)/shard_map/coherence/pallas_call | solution.py:390

commit v2 on v0

v2 whole, which is shorter than its diff:
```python
import jax
import jax.numpy as jnp
import numpy as np
from jax import lax
from jax.experimental import pallas as pl
from jax.experimental.pallas import tpu as pltpu
from jax.sharding import PartitionSpec as P

MESH = pl.DeviceIdType.MESH
DATE_DEV = 4
ROWS = 64
COLS = 1024
BLOCKS = COLS // 128
REFS = 3
STEPS = 4
VMEM_LIMIT = 56 * 2**20


def band_matrix():
    k = np.arange(128)[:, None]
    c = np.arange(128)[None, :]
    middle = (k >= c - 10) & (k <= c + 9)
    edge = ((c < 10) & (k >= 118 + c)) | ((c >= 119) & (k <= c - 119))
    half = np.concatenate([middle, edge], axis=1)
    return jnp.asarray(np.concatenate([half, half], axis=0), jnp.bfloat16)


CHIPS = 8


def spread_kernel(
    dates_ref,
    re_ref,
    im_ref,
    refs,
    ref_edges,
    left,
    right,
    own_edges,
    packed,
    outward,
    halves,
    first_half,
    merged,
    pieces,
    pair_send,
    pair_recv,
    edge_send,
    edge_recv,
    first_send,
    first_recv,
    gather_send,
    gather_recv,
    spread_send,
    spread_recv,
    inward_send,
    inward_recv,
    rim_send,
    rim_recv,
    rim_in_send,
    rim_in_recv,
):
    me = lax.axis_index("date")
    tile = lax.axis_index("tile")
    chip, core = me // 2, me % 2
    tiles = lax.axis_size("tile")
    next_tile = {"tile": lax.rem(tile + 1, tiles)}
    last_tile = {"tile": lax.rem(tile + tiles - 1, tiles)}
    sibling = {"date": chip * 2 + 1 - core}

    def same_core(k):
        return {"date": k * 2 + core}

    def other(i):
        return lax.rem(chip + i, CHIPS)

    def remote(source, target, send, recv, to):
        return pltpu.make_async_remote_copy(src_ref=source, dst_ref=target, send_sem=send, recv_sem=recv, device_id=to, device_id_type=MESH)

    barrier = pltpu.get_barrier_semaphore()

    def greet(target):
        pl.semaphore_signal(barrier, inc=1, device_id=target, device_id_type=MESH)

    @pl.loop(1, CHIPS)
    def _(i):
        greet(same_core(other(i)))

    greet(next_tile)
    greet(last_tile)
    greet(sibling)

    def half(slot, c):
        rows = pl.ds(pl.multiple_of(c * 32, 32), 32)
        return re_ref[slot, rows].reshape(4, 8, COLS), im_ref[slot, rows].reshape(4, 8, COLS)

    for s in range(1, REFS):
        slot = lax.rem(dates_ref[s], DATE_DEV)
        halves[core, s - 1, 0:4], halves[core, s - 1, 4:8] = half(slot, core)
        outward[s - 1, 0:4], outward[s - 1, 4:8] = half(slot, 1 - core)

    @pl.when(me == 0)
    def _():
        first_half[0:4], first_half[4:8] = half(0, 0)
        outward[REFS - 1, 0:4], outward[REFS - 1, 4:8] = half(0, 1)

    for j in range(DATE_DEV):
        own_edges[j, 0:2] = re_ref[j, 0:2]
        own_edges[j, 2:4] = re_ref[j, ROWS - 2 : ROWS]
        own_edges[j, 4:6] = im_ref[j, 0:2]
        own_edges[j, 6:8] = im_ref[j, ROWS - 2 : ROWS]

    pl.semaphore_wait(barrier, 10)

    to_sibling = remote(outward.at[pl.ds(0, 2)], halves.at[core], pair_send.at[0], pair_recv.at[0], sibling)
    first_to_sibling = remote(outward.at[REFS - 1], first_half, pair_send.at[1], pair_recv.at[1], sibling)
    to_sibling.start()

    def first_out(k):
        return remote(first_half.at[k], refs.at[0, core, k], first_send.at[k], first_recv.at[0], same_core(k))

    def first_all():
        refs[0, core, 0] = first_half[0]

        @pl.loop(1, CHIPS)
        def _(k):
            first_out(k).start()

    @pl.when(me == 0)
    def _():
        first_to_sibling.start()
        first_all()

    to_right = remote(own_edges, left, edge_send.at[0], edge_recv.at[0], next_tile)
    to_left = remote(own_edges, right, edge_send.at[1], edge_recv.at[1], last_tile)
    to_right.start()
    to_left.start()

    to_sibling.wait_recv()
    for s in range(1, REFS):
        owner_core = lax.rem(dates_ref[s] // DATE_DEV, 2)
        merged[:, s - 1] = halves[owner_core, s - 1]

    def gather(k):
        return remote(merged.at[k], pieces.at[chip], gather_send.at[k], gather_recv.at[chip], same_core(k))

    def gathered(k):
        return remote(merged.at[k], pieces.at[k], gather_send.at[k], gather_recv.at[k], same_core(k))

    @pl.loop(1, CHIPS)
    def _(i):
        gather(other(i)).start()

    @pl.when(me == 1)
    def _():
        first_to_sibling.wait_recv()
        first_all()

    def part(n, k):
        return refs.at[0, core, k] if n == 0 else refs.at[pl.ds(1, 2), core, k]

    def spread_out(n, k):
        return remote(part(n, chip), part(n, chip), spread_send.at[n, k], spread_recv.at[n, chip], same_core(k))

    def spread_in(n, k):
        return remote(part(n, k), part(n, k), spread_send.at[n, k], spread_recv.at[n, k], same_core(k))

    def inward(n, k):
        return remote(part(n, k), part(n, k), inward_send.at[n, k], inward_recv.at[n, k], sibling)

    def inward_in(n, k):
        there = refs.at[0, 1 - core, k] if n == 0 else refs.at[pl.ds(1, 2), 1 - core, k]
        return remote(there, there, inward_send.at[n, k], inward_recv.at[n, k], sibling)

    def spread_all(n):
        @pl.loop(1, CHIPS)
        def _(i):
            spread_out(n, other(i)).start()

        inward(n, chip).start()

    @pl.when(chip > 0)
    def _():
        first_out(chip).wait_recv()

    spread_all(0)
    pieces[chip] = merged[chip]

    @pl.loop(1, CHIPS)
    def _(i):
        gathered(other(i)).wait_recv()

    for s in range(1, REFS):
        refs[s, core, chip] = pieces[dates_ref[s] // (2 * DATE_DEV), s - 1]
    spread_all(1)

    below = (core == 0) & (lax.rem(chip, 4) == 0)
    above = (core == 1) & (lax.rem(chip, 4) == 3)
    own_kind = jnp.where(core == 0, 0, 2) + chip // 4

    def rim_over(to):
        return remote(packed, ref_edges.at[own_kind], rim_send.at[0], rim_recv.at[4], to)

    @pl.when(below)
    def _():
        for s in range(REFS):
            packed[2 * s : 2 * s + 2] = refs[s, core, chip, 0:2]
        packed[6:8] = jnp.zeros((2, COLS), jnp.float32)
        rim_over(last_tile).start()

    @pl.when(above)
    def _():
        for s in range(REFS):
            packed[2 * s : 2 * s + 2] = refs[s, core, chip, 6:8]
        packed[6:8] = jnp.zeros((2, COLS), jnp.float32)
        rim_over(next_tile).start()

    def rim_out(k):
        return remote(ref_edges.at[own_kind], ref_edges.at[own_kind], rim_send.at[1 + k], rim_recv.at[own_kind], same_core(k))

    def rim_in(kind):
        return remote(ref_edges.at[kind], ref_edges.at[kind], rim_send.at[0], rim_recv.at[kind], sibling)

    def rim_inward(kind):
        return remote(ref_edges.at[kind], ref_edges.at[kind], rim_in_send.at[kind], rim_in_recv.at[kind], sibling)

    @pl.when(below | above)
    def _():
        rim_over(next_tile).wait_recv()

        @pl.loop(1, CHIPS)
        def _(i):
            rim_out(other(i)).start()

        rim_inward(own_kind).start()

    for n in range(2):

        @pl.loop(1, CHIPS)
        def _(i):
            k = other(i)
            spread_in(n, k).wait_recv()
            inward(n, k).start()

    @pl.loop(0, 2)
    def _(m):
        kind = core * 2 + m

        @pl.when(jnp.logical_not((below | above) & (kind == own_kind)))
        def _():
            rim_in(kind).wait_recv()
            rim_inward(kind).start()

    for n in range(2):

        @pl.loop(0, CHIPS)
        def _(k):
            inward_in(n, k).wait_recv()

    @pl.loop(0, 2)
    def _(m):
        rim_inward((1 - core) * 2 + m).wait_recv()
        rim_inward(core * 2 + m).wait_send()

    to_right.wait()
    to_left.wait()
    to_sibling.wait_send()

    @pl.when(me == 0)
    def _():
        first_to_sibling.wait_send()

    @pl.when(chip == 0)
    def _():
        @pl.loop(1, CHIPS)
        def _(k):
            first_out(k).wait_send()

    @pl.when(below | above)
    def _():
        rim_over(next_tile).wait_send()

        @pl.loop(1, CHIPS)
        def _(i):
            rim_out(other(i)).wait_send()

    @pl.loop(1, CHIPS)
    def _(i):
        gather(other(i)).wait_send()

    for n in range(2):

        @pl.loop(1, CHIPS)
        def _(i):
            spread_out(n, other(i)).wait_send()
            inward(n, other(i)).wait_send()

        inward(n, chip).wait_send()


def spread(dates, slc_re, slc_im):
    vmem = pl.BlockSpec(memory_space=pltpu.VMEM)
    f32 = jnp.float32
    dma = pltpu.SemaphoreType.DMA
    return pl.pallas_call(
        spread_kernel,
        out_shape=(
            jax.ShapeDtypeStruct((REFS, 2, CHIPS, 8, COLS), f32),
            jax.ShapeDtypeStruct((4, 8, COLS), f32),
            jax.ShapeDtypeStruct((DATE_DEV, 8, COLS), f32),
            jax.ShapeDtypeStruct((DATE_DEV, 8, COLS), f32),
        ),
        in_specs=[pl.BlockSpec(memory_space=pltpu.SMEM), vmem, vmem],
        out_specs=(vmem, vmem, vmem, vmem),
        scratch_shapes=[
            pltpu.VMEM((DATE_DEV, 8, COLS), f32),
            pltpu.VMEM((8, COLS), f32),
            pltpu.VMEM((REFS, CHIPS, 8, COLS), f32),
            pltpu.VMEM((2, 2, CHIPS, 8, COLS), f32),
            pltpu.VMEM((CHIPS, 8, COLS), f32),
            pltpu.VMEM((CHIPS, 2, 8, COLS), f32),
            pltpu.VMEM((CHIPS, 2, 8, COLS), f32),
            dma((2,)),
            dma((2,)),
            dma((2,)),
            dma((2,)),
            dma((CHIPS,)),
            dma((1,)),
            dma((CHIPS,)),
            dma((CHIPS,)),
            dma((2, CHIPS)),
            dma((2, CHIPS)),
            dma((2, CHIPS)),
            dma((2, CHIPS)),
            dma((CHIPS + 1,)),
            dma((5,)),
            dma((4,)),
            dma((4,)),
        ],
        compiler_params=pltpu.CompilerParams(collective_id=0, has_side_effects=True, vmem_limit_bytes=VMEM_LIMIT),
        name="spread",
    )(dates, slc_re, slc_im)


def compute_kernel(
    dates_ref,
    keep_ref,
    offsets_ref,
    re_hbm,
    im_hbm,
    left_hbm,
    right_hbm,
    refs_hbm,
    ref_edges_hbm,
    band,
    out_re,
    out_im,
    re_ref,
    im_ref,
    left,
    right,
    refs,
    ref_edges,
    zeros,
    stage,
    a_ext,
    b_ext,
    prod,
    wide,
    pow_a,
    pow_b,
    date_sems,
    edge_sems,
    ref_sems,
    out_sems,
):
    me = lax.axis_index("date")
    tile = lax.axis_index("tile")
    has_top = (tile > 0).astype(jnp.float32)
    has_bottom = (tile < lax.axis_size("tile") - 1).astype(jnp.float32)
    outs = (out_re, out_im)

    def edge_loads():
        sources = ((left_hbm, left), (right_hbm, right), (ref_edges_hbm, ref_edges))
        return [pltpu.make_async_copy(a, b, edge_sems.at[k]) for k, (a, b) in enumerate(sources)]

    def date_loads(j):
        sources = ((re_hbm, re_ref), (im_hbm, im_ref))
        return [pltpu.make_async_copy(a.at[j], b.at[j], date_sems.at[k, j]) for k, (a, b) in enumerate(sources)]

    def ref_load(s):
        return pltpu.make_async_copy(refs_hbm.at[s], refs.at[s], ref_sems.at[s])

    def zero_out(s, j, p):
        return pltpu.make_async_copy(zeros, outs[p].at[s, j], out_sems.at[p, s, j])

    def value_out(s, j, p):
        return pltpu.make_async_copy(stage.at[p, s, j], outs[p].at[s, j], out_sems.at[p, s, j])

    def valid(s, j):
        date = me * DATE_DEV + j
        return (keep_ref[s, date] == 1) & (date > dates_ref[s])

    for c in edge_loads():
        c.start()

    @pl.loop(0, DATE_DEV)
    def _(j):
        for c in date_loads(j):
            c.start()

    @pl.loop(0, REFS)
    def _(s):
        ref_load(s).start()

    zeros[...] = jnp.zeros_like(zeros)

    @pl.loop(0, STEPS)
    def _(s):
        @pl.loop(0, DATE_DEV)
        def _(j):
            @pl.when(jnp.logical_not(valid(s, j)))
            def _():
                zero_out(s, j, 0).start()
                zero_out(s, j, 1).start()

    def lay(ext, plane, rows, top, bottom):
        top = top * has_top
        bottom = bottom * has_bottom
        for g in range(BLOCKS):
            cut = slice(128 * g, 128 * g + 128)
            ext[plane, g, 0:2] = top[:, cut]
            ext[plane, g, 2 : ROWS + 2] = rows[:, cut]
            ext[plane, g, ROWS + 2 : ROWS + 4] = bottom[:, cut]

    def edge_rows(tile_rows, at):
        return jnp.where(at == 0, tile_rows[0:2], jnp.where(at == 1, tile_rows[2:4], tile_rows[4:6]))

    def widen(count):
        for g in range(BLOCKS):
            for p in range(count):
                total = prod[p, g, 0:ROWS]
                for k in range(1, 5):
                    total = total + prod[p, g, k : k + ROWS]
                high = total.astype(jnp.bfloat16)
                low = (total - high.astype(jnp.float32)).astype(jnp.bfloat16)
                wide[g, p * ROWS : (p + 1) * ROWS, 0:128] = high
                wide[g, p * ROWS : (p + 1) * ROWS, 128:256] = low

    def columns(count):
        rows = count * ROWS
        lhs = wide[:, 0:rows, :].reshape(BLOCKS * rows, 256)
        return jnp.dot(lhs, band[...], preferred_element_type=jnp.float32).reshape(BLOCKS, rows, 256)

    lane = lax.broadcasted_iota(jnp.int32, (ROWS, 128), 1)

    def joined(sums, g, p):
        rows = slice(p * ROWS, (p + 1) * ROWS)
        zero = jnp.zeros((ROWS, 128), jnp.float32)
        before = sums[g - 1, rows, 128:256] if g > 0 else zero
        after = sums[g + 1, rows, 128:256] if g < BLOCKS - 1 else zero
        return sums[g, rows, 0:128] + jnp.where(lane < 64, before, after)

    def power(ext, out):
        for g in range(BLOCKS):
            prod[0, g] = ext[0, g] * ext[0, g] + ext[1, g] * ext[1, g]
        widen(1)
        sums = columns(1)
        for g in range(BLOCKS):
            out[g] = joined(sums, g, 0)

    def pair(s, j):
        for g in range(BLOCKS):
            a_re, a_im = a_ext[0, g], a_ext[1, g]
            b_re, b_im = b_ext[j, 0, g], b_ext[j, 1, g]
            prod[0, g] = a_re * b_re + a_im * b_im
            prod[1, g] = a_im * b_re - a_re * b_im
        widen(2)
        sums = columns(2)
        for g in range(BLOCKS):
            scale = lax.rsqrt(pow_a[g] * pow_b[j, g] + 1e-06)
            for p in range(2):
                stage[p, s, j, :, 128 * g : 128 * g + 128] = joined(sums, g, p) * scale
        value_out(s, j, 0).start()
        value_out(s, j, 1).start()

    for c in edge_loads():
        c.wait()

    @pl.loop(0, DATE_DEV)
    def _(j):
        for c in date_loads(j):
            c.wait()
        offset = offsets_ref[me * DATE_DEV + j]
        turn = lax.rem(COLS - offset, COLS)

        def shifted(x):
            column = lax.broadcasted_iota(jnp.int32, x.shape, 1)
            return jnp.where(column < COLS - offset, pltpu.roll(x, turn, 1), 0.0)

        edges_left = shifted(left[j])
        edges_right = shifted(right[j])
        lay(b_ext.at[j], 0, shifted(re_ref[j]), edges_left[2:4], edges_right[0:2])
        lay(b_ext.at[j], 1, shifted(im_ref[j]), edges_left[6:8], edges_right[4:6])
        power(b_ext.at[j], pow_b.at[j])

    @pl.loop(0, STEPS)
    def _(s):
        @pl.when(s < REFS)
        def _():
            at = jnp.minimum(s, REFS - 1)
            ref_load(at).wait()
            for p in range(2):
                rows = refs[at, :, 4 * p : 4 * p + 4].reshape(ROWS, COLS)
                lay(a_ext, p, rows, edge_rows(ref_edges[2 + p], at), edge_rows(ref_edges[p], at))

        @pl.when(s == REFS)
        def _():
            edges_left = left[DATE_DEV - 2]
            edges_right = right[DATE_DEV - 2]
            lay(a_ext, 0, re_ref[DATE_DEV - 2], edges_left[2:4], edges_right[0:2])
            lay(a_ext, 1, im_ref[DATE_DEV - 2], edges_left[6:8], edges_right[4:6])

        some = valid(s, 0) | valid(s, 1) | valid(s, 2) | valid(s, 3)

        @pl.when(some)
        def _():
            power(a_ext, pow_a)

        @pl.loop(0, DATE_DEV)
        def _(j):
            @pl.when(valid(s, j))
            def _():
                pair(s, j)

    @pl.loop(0, STEPS)
    def _(s):
        @pl.loop(0, DATE_DEV)
        def _(j):
            value_out(s, j, 0).wait()
            value_out(s, j, 1).wait()


def compute(dates, keep, offsets, slc_re, slc_im, left, right, refs, ref_edges):
    smem = pl.BlockSpec(memory_space=pltpu.SMEM)
    vmem = pl.BlockSpec(memory_space=pltpu.VMEM)
    hbm = pl.BlockSpec(memory_space=pl.ANY)
    shape = jax.ShapeDtypeStruct((STEPS, DATE_DEV, ROWS, COLS), jnp.float32)
    f32 = jnp.float32
    return pl.pallas_call(
        compute_kernel,
        out_shape=(shape, shape),
        in_specs=[smem] * 3 + [hbm] * 6 + [vmem],
        out_specs=(hbm, hbm),
        scratch_shapes=[
            pltpu.VMEM((DATE_DEV, ROWS, COLS), f32),
            pltpu.VMEM((DATE_DEV, ROWS, COLS), f32),
            pltpu.VMEM((DATE_DEV, 8, COLS), f32),
            pltpu.VMEM((DATE_DEV, 8, COLS), f32),
            pltpu.VMEM((REFS, 2, CHIPS, 8, COLS), f32),
            pltpu.VMEM((4, 8, COLS), f32),
            pltpu.VMEM((ROWS, COLS), f32),
            pltpu.VMEM((2, STEPS, DATE_DEV, ROWS, COLS), f32),
            pltpu.VMEM((2, BLOCKS, 72, 128), f32),
            pltpu.VMEM((DATE_DEV, 2, BLOCKS, 72, 128), f32),
            pltpu.VMEM((2, BLOCKS, 72, 128), f32),
            pltpu.VMEM((BLOCKS, 2 * ROWS, 256), jnp.bfloat16),
            pltpu.VMEM((BLOCKS, ROWS, 128), f32),
            pltpu.VMEM((DATE_DEV, BLOCKS, ROWS, 128), f32),
            pltpu.SemaphoreType.DMA((2, DATE_DEV)),
            pltpu.SemaphoreType.DMA((3,)),
            pltpu.SemaphoreType.DMA((REFS,)),
            pltpu.SemaphoreType.DMA((2, STEPS, DATE_DEV)),
        ],
        compiler_params=pltpu.CompilerParams(vmem_limit_bytes=VMEM_LIMIT),
        name="coherence",
    )(dates, keep, offsets, slc_re, slc_im, left, right, refs, ref_edges, band_matrix())


def body(slc_re, slc_im, ref_dates, pair_keep, col_offsets):
    refs, ref_edges, left, right = spread(ref_dates, slc_re, slc_im)
    return compute(ref_dates, pair_keep, col_offsets, slc_re, slc_im, left, right, refs, ref_edges)


def solution(mesh):
    placed = (P("date", "tile", None), P("date", "tile", None), P(), P(), P())
    return jax.shard_map(
        body,
        mesh=mesh,
        in_specs=placed,
        out_specs=(P(None, "date", "tile", None), P(None, "date", "tile", None)),
        check_vma=False,
    )
```

time: 468 us -> 48.1 us (0.10)
  the two profiles are of different devices: /device:TPU:8 before, /device:TPU:1 now
where the time goes in v2:
time: 48.1 us; the launch traced here: 47.6 us
  Pallas kernels  47 us (98%)
  between operations  0.64 us (1%)
    pallas_call x1, Pallas kernels, spread(): pl.pallas_call(spread_kernel, out_shape=(jax.ShapeDtypeStruct((REFS, 2, C...  39.1 us
    pallas_call x1, Pallas kernels, compute(): pl.pallas_call(compute_kernel, out_shape=(shape, shape), in_specs=[smem]...  7.86 us

profile of v2, /device:TPU:1, one launch (start us, length us, event | category | flops | bytes accessed | tf_op | source)
XLA Modules:
  0.0 47.6 jit_solution(3494426397108351249)
XLA Ops:
  0.6 39.1 %spread.1 = (f32[3,2,8,8,1024]{4,3,2,1,0:T(8,128)}, f32[4,8,1024]{2,1,0:T(8,128)}, f32[4,8,1024]{2,1,0:T(8,128)}, f32[4,8,1024]{2,1,0:T(8,128)}) custom-call(s32[4]{0:T(128)} %dates_ref.3, f32[4,64,1024]{2,1,0:T(8,128)} %re_hbm.1, f32[4,64,1024]{2,1,0:T(8,128)} %im_hbm.1), custom_call_target="tpu_custom_call" | custom-call | tf_op jit(solution)/shard_map/spread/pallas_call | solution.py:305
  39.8 7.9 %coherence.1 = (f32[4,4,64,1024]{3,2,1,0:T(8,128)}, f32[4,4,64,1024]{3,2,1,0:T(8,128)}) custom-call(s32[4]{0:T(128)} %dates_ref.3, s32[4,64]{1,0:T(4,128)} %keep_ref.1, s32[64]{0:T(128)} %offsets_ref.1, f32[4,64,1024]{2,1,0:T(8,128)} %re_hbm.1, f32[4,64,1024]{2,1,0:T(8,128)} %im_hbm.1, f32[4,8,1024]{2,1,0:T(8,128)} %get-tuple-element.6.left_hbm, ...), custom_call_target="tpu_custom_call" | custom-call | tf_op jit(solution)/shard_map/coherence/pallas_call | solution.py:550

commit v3 on v2

--- a/solution.py
+++ b/solution.py
@@ -1,6 +1,5 @@
 import jax
 import jax.numpy as jnp
-import numpy as np
 from jax import lax
 from jax.experimental import pallas as pl
 from jax.experimental.pallas import tpu as pltpu
@@ -13,29 +12,98 @@
 BLOCKS = COLS // 128
 REFS = 3
 STEPS = 4
-VMEM_LIMIT = 56 * 2**20
+VMEM_LIMIT = 24 * 2**20
 
 
 def band_matrix():
-    k = np.arange(128)[:, None]
-    c = np.arange(128)[None, :]
-    middle = (k >= c - 10) & (k <= c + 9)
-    edge = ((c < 10) & (k >= 118 + c)) | ((c >= 119) & (k <= c - 119))
-    half = np.concatenate([middle, edge], axis=1)
-    return jnp.asarray(np.concatenate([half, half], axis=0), jnp.bfloat16)
+    k = lax.rem(lax.broadcasted_iota(jnp.int32, (256, 256), 0), 128)
+    c = lax.broadcasted_iota(jnp.int32, (256, 256), 1)
+    within = (c < 128) & (k >= c - 10) & (k <= c + 9)
+    after = (c >= 128) & (c < 138) & (k >= c - 10)
+    before = (c >= 247) & (k <= c - 247)
+    return jnp.where(within | after | before, 1.0, 0.0).astype(jnp.bfloat16)
+
+
+def lay(ext, plane, rows, top, bottom):
+    for g in range(BLOCKS):
+        cut = slice(128 * g, 128 * g + 128)
+        ext[plane, g, 0:2] = top[:, cut]
+        ext[plane, g, 2 : ROWS + 2] = rows[:, cut]
+        ext[plane, g, ROWS + 2 : ROWS + 4] = bottom[:, cut]
+
+
+def widen(prod, wide, count):
+    for g in range(BLOCKS):
+        for p in range(count):
+            total = prod[p, g, 0:ROWS]
+            for k in range(1, 5):
+                total = total + prod[p, g, k : k + ROWS]
+            high = total.astype(jnp.bfloat16)
+            low = (total - high.astype(jnp.float32)).astype(jnp.bfloat16)
+            wide[g, p * ROWS : (p + 1) * ROWS, 0:128] = high
+            wide[g, p * ROWS : (p + 1) * ROWS, 128:256] = low
+
+
+def columns(wide, band, count):
+    rows = count * ROWS
+    lhs = wide[:, 0:rows, :].reshape(BLOCKS * rows, 256)
+    return jnp.dot(lhs, band[...], preferred_element_type=jnp.float32).reshape(BLOCKS, rows, 256)
+
+
+def joined(sums, g, p):
+    lane = lax.broadcasted_iota(jnp.int32, (ROWS, 128), 1)
+    rows = slice(p * ROWS, (p + 1) * ROWS)
+    zero = jnp.zeros((ROWS, 128), jnp.float32)
+    before = sums[g - 1, rows, 128:256] if g > 0 else zero
+    after = sums[g + 1, rows, 128:256] if g < BLOCKS - 1 else zero
+    return sums[g, rows, 0:128] + jnp.where(lane < 64, before, after)
+
+
+def power(ext, out, prod, wide, band):
+    for g in range(BLOCKS):
+        prod[0, g] = ext[0, g] * ext[0, g] + ext[1, g] * ext[1, g]
+    widen(prod, wide, 1)
+    sums = columns(wide, band, 1)
+    for g in range(BLOCKS):
+        out[g] = joined(sums, g, 0)
+
+
+def coherence(a_ext, pow_a, b_ext, pow_b, out_re, out_im, prod, wide, band):
+    for g in range(BLOCKS):
+        a_re, a_im = a_ext[0, g], a_ext[1, g]
+        b_re, b_im = b_ext[0, g], b_ext[1, g]
+        prod[0, g] = a_re * b_re + a_im * b_im
+        prod[1, g] = a_im * b_re - a_re * b_im
+    widen(prod, wide, 2)
+    sums = columns(wide, band, 2)
+    for g in range(BLOCKS):
+        scale = lax.rsqrt(pow_a[g] * pow_b[g] + 1e-06)
+        for p, out in ((0, out_re), (1, out_im)):
+            out[:, 128 * g : 128 * g + 128] = joined(sums, g, p) * scale
 
 
 CHIPS = 8
 
 
 def spread_kernel(
-    dates_ref,
-    re_ref,
-    im_ref,
+    dates_hbm,
+    offsets_hbm,
+    re_hbm,
+    im_hbm,
     refs,
     ref_edges,
     left,
     right,
+    b_ext,
+    pow_b,
+    dates_ref,
+    offsets_ref,
+    re_ref,
+    im_ref,
+    band,
+    prod,
+    wide,
+    load_sems,
     own_edges,
     packed,
     outward,
@@ -77,6 +145,11 @@
     def remote(source, target, send, recv, to):
         return pltpu.make_async_remote_copy(src_ref=source, dst_ref=target, send_sem=send, recv_sem=recv, device_id=to, device_id_type=MESH)
 
+    sources = ((dates_hbm, dates_ref), (offsets_hbm, offsets_ref), (re_hbm, re_ref), (im_hbm, im_ref))
+    loads = [pltpu.make_async_copy(a, b, load_sems.at[k]) for k, (a, b) in enumerate(sources)]
+    for c in loads:
+        c.start()
+
     barrier = pltpu.get_barrier_semaphore()
 
     def greet(target):
@@ -89,6 +162,10 @@
     greet(next_tile)
     greet(last_tile)
     greet(sibling)
+    band[...] = band_matrix()
+
+    for c in loads:
+        c.wait()
 
     def half(slot, c):
         rows = pl.ds(pl.multiple_of(c * 32, 32), 32)
@@ -186,13 +263,33 @@
     spread_all(0)
     pieces[chip] = merged[chip]
 
+    to_right.wait()
+    to_left.wait()
+    has_top = (tile > 0).astype(jnp.float32)
+    has_bottom = (tile < tiles - 1).astype(jnp.float32)
+
+    @pl.loop(0, DATE_DEV)
+    def _(j):
+        offset = offsets_ref[me * DATE_DEV + j]
+
+        def shifted(x):
+            for step in (1, 2, 4):
+                x = jnp.where(lax.rem(offset // step, 2) == 1, pltpu.roll(x, COLS - step, 1), x)
+            column = lax.broadcasted_iota(jnp.int32, x.shape, 1)
+            return jnp.where(column < COLS - offset, x, 0.0)
+
+        above_rows = shifted(left[j]) * has_top
+        below_rows = shifted(right[j]) * has_bottom
+        lay(b_ext.at[j], 0, shifted(re_ref[j]), above_rows[2:4], below_rows[0:2])
+        lay(b_ext.at[j], 1, shifted(im_ref[j]), above_rows[6:8], below_rows[4:6])
+        power(b_ext.at[j], pow_b.at[j], prod, wide, band)
+
     @pl.loop(1, CHIPS)
     def _(i):
         gathered(other(i)).wait_recv()
 
     for s in range(1, REFS):
         refs[s, core, chip] = pieces[dates_ref[s] // (2 * DATE_DEV), s - 1]
-    spread_all(1)
 
     below = (core == 0) & (lax.rem(chip, 4) == 0)
     above = (core == 1) & (lax.rem(chip, 4) == 3)
@@ -214,6 +311,8 @@
             packed[2 * s : 2 * s + 2] = refs[s, core, chip, 6:8]
         packed[6:8] = jnp.zeros((2, COLS), jnp.float32)
         rim_over(next_tile).start()
+
+    spread_all(1)
 
     def rim_out(k):
         return remote(ref_edges.at[own_kind], ref_edges.at[own_kind], rim_send.at[1 + k], rim_recv.at[own_kind], same_core(k))
@@ -262,8 +361,6 @@
         rim_inward((1 - core) * 2 + m).wait_recv()
         rim_inward(core * 2 + m).wait_send()
 
-    to_right.wait()
-    to_left.wait()
     to_sibling.wait_send()
 
     @pl.when(me == 0)
@@ -298,8 +395,10 @@
         inward(n, chip).wait_send()
 
 
-def spread(dates, slc_re, slc_im):
+def spread(dates, offsets, slc_re, slc_im):
     vmem = pl.BlockSpec(memory_space=pltpu.VMEM)
+    hbm = pl.BlockSpec(memory_space=pltpu.HBM)
+    dates_all = offsets.shape[0]
     f32 = jnp.float32
     dma = pltpu.SemaphoreType.DMA
     return pl.pallas_call(
@@ -309,10 +408,20 @@
             jax.ShapeDtypeStruct((4, 8, COLS), f32),
             jax.ShapeDtypeStruct((DATE_DEV, 8, COLS), f32),
             jax.ShapeDtypeStruct((DATE_DEV, 8, COLS), f32),
+            jax.ShapeDtypeStruct((DATE_DEV, 2, BLOCKS, 72, 128), f32),
+            jax.ShapeDtypeStruct((DATE_DEV, BLOCKS, ROWS, 128), f32),
         ),
-        in_specs=[pl.BlockSpec(memory_space=pltpu.SMEM), vmem, vmem],
-        out_specs=(vmem, vmem, vmem, vmem),
+        in_specs=[hbm] * 4,
+        out_specs=(vmem,) * 6,
         scratch_shapes=[
+            pltpu.SMEM((STEPS,), jnp.int32),
+            pltpu.SMEM((dates_all,), jnp.int32),
+            pltpu.VMEM((DATE_DEV, ROWS, COLS), f32),
+            pltpu.VMEM((DATE_DEV, ROWS, COLS), f32),
+            pltpu.VMEM((256, 256), jnp.bfloat16),
+            pltpu.VMEM((2, BLOCKS, 72, 128), f32),
+            pltpu.VMEM((BLOCKS, 2 * ROWS, 256), jnp.bfloat16),
+            dma((4,)),
             pltpu.VMEM((DATE_DEV, 8, COLS), f32),
             pltpu.VMEM((8, COLS), f32),
             pltpu.VMEM((REFS, CHIPS, 8, COLS), f32),
@@ -339,39 +448,33 @@
         ],
         compiler_params=pltpu.CompilerParams(collective_id=0, has_side_effects=True, vmem_limit_bytes=VMEM_LIMIT),
         name="spread",
-    )(dates, slc_re, slc_im)
+    )(dates, offsets, slc_re, slc_im)
 
 
 def compute_kernel(
-    dates_ref,
-    keep_ref,
-    offsets_ref,
+    dates_hbm,
+    keep_hbm,
     re_hbm,
     im_hbm,
-    left_hbm,
-    right_hbm,
-    refs_hbm,
-    ref_edges_hbm,
-    band,
-    out_re,
-    out_im,
-    re_ref,
-    im_ref,
     left,
     right,
     refs,
     ref_edges,
+    b_ext,
+    pow_b,
+    out_re,
+    out_im,
+    dates_ref,
+    keep_ref,
+    band,
+    own,
     zeros,
     stage,
     a_ext,
-    b_ext,
     prod,
     wide,
     pow_a,
-    pow_b,
-    date_sems,
-    edge_sems,
-    ref_sems,
+    own_sems,
     out_sems,
 ):
     me = lax.axis_index("date")
@@ -380,17 +483,6 @@
     has_bottom = (tile < lax.axis_size("tile") - 1).astype(jnp.float32)
     outs = (out_re, out_im)
 
-    def edge_loads():
-        sources = ((left_hbm, left), (right_hbm, right), (ref_edges_hbm, ref_edges))
-        return [pltpu.make_async_copy(a, b, edge_sems.at[k]) for k, (a, b) in enumerate(sources)]
-
-    def date_loads(j):
-        sources = ((re_hbm, re_ref), (im_hbm, im_ref))
-        return [pltpu.make_async_copy(a.at[j], b.at[j], date_sems.at[k, j]) for k, (a, b) in enumerate(sources)]
-
-    def ref_load(s):
-        return pltpu.make_async_copy(refs_hbm.at[s], refs.at[s], ref_sems.at[s])
-
     def zero_out(s, j, p):
         return pltpu.make_async_copy(zeros, outs[p].at[s, j], out_sems.at[p, s, j])
 
@@ -401,19 +493,14 @@
         date = me * DATE_DEV + j
         return (keep_ref[s, date] == 1) & (date > dates_ref[s])
 
-    for c in edge_loads():
+    scalars = ((dates_hbm, dates_ref), (keep_hbm, keep_ref))
+    loads = [pltpu.make_async_copy(a, b, own_sems.at[2 + k]) for k, (a, b) in enumerate(scalars)]
+    for c in loads:
         c.start()
-
-    @pl.loop(0, DATE_DEV)
-    def _(j):
-        for c in date_loads(j):
-            c.start()
-
-    @pl.loop(0, REFS)
-    def _(s):
-        ref_load(s).start()
-
     zeros[...] = jnp.zeros_like(zeros)
+    band[...] = band_matrix()
+    for c in loads:
+        c.wait()
 
     @pl.loop(0, STEPS)
     def _(s):
@@ -424,114 +511,46 @@
                 zero_out(s, j, 0).start()
                 zero_out(s, j, 1).start()
 
-    def lay(ext, plane, rows, top, bottom):
-        top = top * has_top
-        bottom = bottom * has_bottom
-        for g in range(BLOCKS):
-            cut = slice(128 * g, 128 * g + 128)
-            ext[plane, g, 0:2] = top[:, cut]
-            ext[plane, g, 2 : ROWS + 2] = rows[:, cut]
-            ext[plane, g, ROWS + 2 : ROWS + 4] = bottom[:, cut]
-
     def edge_rows(tile_rows, at):
         return jnp.where(at == 0, tile_rows[0:2], jnp.where(at == 1, tile_rows[2:4], tile_rows[4:6]))
 
-    def widen(count):
-        for g in range(BLOCKS):
-            for p in range(count):
-                total = prod[p, g, 0:ROWS]
-                for k in range(1, 5):
-                    total = total + prod[p, g, k : k + ROWS]
-                high = total.astype(jnp.bfloat16)
-                low = (total - high.astype(jnp.float32)).astype(jnp.bfloat16)
-                wide[g, p * ROWS : (p + 1) * ROWS, 0:128] = high
-                wide[g, p * ROWS : (p + 1) * ROWS, 128:256] = low
-
-    def columns(count):
-        rows = count * ROWS
-        lhs = wide[:, 0:rows, :].reshape(BLOCKS * rows, 256)
-        return jnp.dot(lhs, band[...], preferred_element_type=jnp.float32).reshape(BLOCKS, rows, 256)
-
-    lane = lax.broadcasted_iota(jnp.int32, (ROWS, 128), 1)
-
-    def joined(sums, g, p):
-        rows = slice(p * ROWS, (p + 1) * ROWS)
-        zero = jnp.zeros((ROWS, 128), jnp.float32)
-        before = sums[g - 1, rows, 128:256] if g > 0 else zero
-        after = sums[g + 1, rows, 128:256] if g < BLOCKS - 1 else zero
-        return sums[g, rows, 0:128] + jnp.where(lane < 64, before, after)
-
-    def power(ext, out):
-        for g in range(BLOCKS):
-            prod[0, g] = ext[0, g] * ext[0, g] + ext[1, g] * ext[1, g]
-        widen(1)
-        sums = columns(1)
-        for g in range(BLOCKS):
-            out[g] = joined(sums, g, 0)
-
-    def pair(s, j):
-        for g in range(BLOCKS):
-            a_re, a_im = a_ext[0, g], a_ext[1, g]
-            b_re, b_im = b_ext[j, 0, g], b_ext[j, 1, g]
-            prod[0, g] = a_re * b_re + a_im * b_im
-            prod[1, g] = a_im * b_re - a_re * b_im
-        widen(2)
-        sums = columns(2)
-        for g in range(BLOCKS):
-            scale = lax.rsqrt(pow_a[g] * pow_b[j, g] + 1e-06)
-            for p in range(2):
-                stage[p, s, j, :, 128 * g : 128 * g + 128] = joined(sums, g, p) * scale
-        value_out(s, j, 0).start()
-        value_out(s, j, 1).start()
-
-    for c in edge_loads():
-        c.wait()
-
-    @pl.loop(0, DATE_DEV)
-    def _(j):
-        for c in date_loads(j):
-            c.wait()
-        offset = offsets_ref[me * DATE_DEV + j]
-        turn = lax.rem(COLS - offset, COLS)
-
-        def shifted(x):
-            column = lax.broadcasted_iota(jnp.int32, x.shape, 1)
-            return jnp.where(column < COLS - offset, pltpu.roll(x, turn, 1), 0.0)
-
-        edges_left = shifted(left[j])
-        edges_right = shifted(right[j])
-        lay(b_ext.at[j], 0, shifted(re_ref[j]), edges_left[2:4], edges_right[0:2])
-        lay(b_ext.at[j], 1, shifted(im_ref[j]), edges_left[6:8], edges_right[4:6])
-        power(b_ext.at[j], pow_b.at[j])
-
     @pl.loop(0, STEPS)
     def _(s):
-        @pl.when(s < REFS)
+        some = valid(s, 0) | valid(s, 1) | valid(s, 2) | valid(s, 3)
+
+        @pl.when(some & (s < REFS))
         def _():
             at = jnp.minimum(s, REFS - 1)
-            ref_load(at).wait()
             for p in range(2):
                 rows = refs[at, :, 4 * p : 4 * p + 4].reshape(ROWS, COLS)
-                lay(a_ext, p, rows, edge_rows(ref_edges[2 + p], at), edge_rows(ref_edges[p], at))
-
-        @pl.when(s == REFS)
+                top = edge_rows(ref_edges[2 + p], at) * has_top
+                bottom = edge_rows(ref_edges[p], at) * has_bottom
+                lay(a_ext, p, rows, top, bottom)
+
+        @pl.when(some & (s == REFS))
         def _():
-            edges_left = left[DATE_DEV - 2]
-            edges_right = right[DATE_DEV - 2]
-            lay(a_ext, 0, re_ref[DATE_DEV - 2], edges_left[2:4], edges_right[0:2])
-            lay(a_ext, 1, im_ref[DATE_DEV - 2], edges_left[6:8], edges_right[4:6])
-
-        some = valid(s, 0) | valid(s, 1) | valid(s, 2) | valid(s, 3)
+            slot = DATE_DEV - 2
+            loads = [pltpu.make_async_copy(h.at[slot], own.at[p], own_sems.at[p]) for p, h in enumerate((re_hbm, im_hbm))]
+            for c in loads:
+                c.start()
+            for c in loads:
+                c.wait()
+            for p in range(2):
+                top = left[slot, 4 * p + 2 : 4 * p + 4] * has_top
+                bottom = right[slot, 4 * p : 4 * p + 2] * has_bottom
+                lay(a_ext, p, own[p], top, bottom)
 
         @pl.when(some)
         def _():
-            power(a_ext, pow_a)
+            power(a_ext, pow_a, prod, wide, band)
 
         @pl.loop(0, DATE_DEV)
         def _(j):
             @pl.when(valid(s, j))
             def _():
-                pair(s, j)
+                coherence(a_ext, pow_a, b_ext.at[j], pow_b.at[j], stage.at[0, s, j], stage.at[1, s, j], prod, wide, band)
+                value_out(s, j, 0).start()
+                value_out(s, j, 1).start()
 
     @pl.loop(0, STEPS)
     def _(s):
@@ -541,45 +560,40 @@
             value_out(s, j, 1).wait()
 
 
-def compute(dates, keep, offsets, slc_re, slc_im, left, right, refs, ref_edges):
-    smem = pl.BlockSpec(memory_space=pltpu.SMEM)
+def compute(dates, keep, slc_re, slc_im, left, right, refs, ref_edges, b_ext, pow_b):
     vmem = pl.BlockSpec(memory_space=pltpu.VMEM)
-    hbm = pl.BlockSpec(memory_space=pl.ANY)
+    hbm = pl.BlockSpec(memory_space=pltpu.HBM)
     shape = jax.ShapeDtypeStruct((STEPS, DATE_DEV, ROWS, COLS), jnp.float32)
     f32 = jnp.float32
     return pl.pallas_call(
         compute_kernel,
         out_shape=(shape, shape),
-        in_specs=[smem] * 3 + [hbm] * 6 + [vmem],
+        in_specs=[hbm] * 4 + [vmem] * 6,
         out_specs=(hbm, hbm),
         scratch_shapes=[
-            pltpu.VMEM((DATE_DEV, ROWS, COLS), f32),
-            pltpu.VMEM((DATE_DEV, ROWS, COLS), f32),
-            pltpu.VMEM((DATE_DEV, 8, COLS), f32),
-            pltpu.VMEM((DATE_DEV, 8, COLS), f32),
-            pltpu.VMEM((REFS, 2, CHIPS, 8, COLS), f32),
-            pltpu.VMEM((4, 8, COLS), f32),
+            pltpu.SMEM((STEPS,), jnp.int32),
+            pltpu.SMEM(keep.shape, jnp.int32),
+            pltpu.VMEM((256, 256), jnp.bfloat16),
+            pltpu.VMEM((2, ROWS, COLS), f32),
             pltpu.VMEM((ROWS, COLS), f32),
             pltpu.VMEM((2, STEPS, DATE_DEV, ROWS, COLS), f32),
             pltpu.VMEM((2, BLOCKS, 72, 128), f32),
-            pltpu.VMEM((DATE_DEV, 2, BLOCKS, 72, 128), f32),
             pltpu.VMEM((2, BLOCKS, 72, 128), f32),
             pltpu.VMEM((BLOCKS, 2 * ROWS, 256), jnp.bfloat16),
             pltpu.VMEM((BLOCKS, ROWS, 128), f32),
-            pltpu.VMEM((DATE_DEV, BLOCKS, ROWS, 128), f32),
-            pltpu.SemaphoreType.DMA((2, DATE_DEV)),
-            pltpu.SemaphoreType.DMA((3,)),
-            pltpu.SemaphoreType.DMA((REFS,)),
+            pltpu.SemaphoreType.DMA((4,)),
             pltpu.SemaphoreType.DMA((2, STEPS, DATE_DEV)),
         ],
         compiler_params=pltpu.CompilerParams(vmem_limit_bytes=VMEM_LIMIT),
         name="coherence",
-    )(dates, keep, offsets, slc_re, slc_im, left, right, refs, ref_edges, band_matrix())
+    )(dates, keep, slc_re, slc_im, left, right, refs, ref_edges, b_ext, pow_b)
 
 
 def body(slc_re, slc_im, ref_dates, pair_keep, col_offsets):
-    refs, ref_edges, left, right = spread(ref_dates, slc_re, slc_im)
-    return compute(ref_dates, pair_keep, col_offsets, slc_re, slc_im, left, right, refs, ref_edges)
+    hbm = [pltpu.with_memory_space_constraint(x, pltpu.HBM) for x in (slc_re, slc_im, ref_dates, pair_keep, col_offsets)]
+    slc_re, slc_im, ref_dates, pair_keep, col_offsets = hbm
+    refs, ref_edges, left, right, b_ext, pow_b = spread(ref_dates, col_offsets, slc_re, slc_im)
+    return compute(ref_dates, pair_keep, slc_re, slc_im, left, right, refs, ref_edges, b_ext, pow_b)
 
 
 def solution(mesh):

time: 48.1 us -> 42.5 us (0.88)
  Pallas kernels: 47 us -> 41.3 us
    pallas_call x1, Pallas kernels: 7.86 us -> 4.37 us  [compute(): pl.pallas_call(compute_kernel, out_shape=(shape, shape), in_specs=[hbm] *...]
    pallas_call x1, Pallas kernels: 39.1 us -> 36.9 us  [spread(): pl.pallas_call(spread_kernel, out_shape=(jax.ShapeDtypeStruct((REFS, 2, C...]
where the time goes in v3:
time: 42.5 us; the launch traced here: 41.9 us
  Pallas kernels  41.3 us (97%)
  between operations  0.64 us (2%)
    pallas_call x1, Pallas kernels, spread(): pl.pallas_call(spread_kernel, out_shape=(jax.ShapeDtypeStruct((REFS, 2, C...  36.9 us
    pallas_call x1, Pallas kernels, compute(): pl.pallas_call(compute_kernel, out_shape=(shape, shape), in_specs=[hbm] *...  4.37 us

profile of v3, /device:TPU:1, one launch (start us, length us, event | category | flops | bytes accessed | tf_op | source)
XLA Modules:
  0.0 41.9 jit_solution(11381017680453420765)
XLA Ops:
  0.6 36.9 %spread.1 = (f32[3,2,8,8,1024]{4,3,2,1,0:T(8,128)S(1)}, f32[4,8,1024]{2,1,0:T(8,128)S(1)}, f32[4,8,1024]{2,1,0:T(8,128)S(1)}, f32[4,8,1024]{2,1,0:T(8,128)S(1)},...) custom-call(s32[4]{0:T(128)} %dates_hbm.3, s32[64]{0:T(128)} %offsets_hbm.1, f32[4,64,1024]{2,1,0:T(8,128)} %re_hbm.3, ...), custom_call_target="tpu_custom_call" | custom-call | tf_op jit(solution)/shard_map/spread/pallas_call | solution.py:404
  37.5 4.4 %coherence.1 = (f32[4,4,64,1024]{3,2,1,0:T(8,128)}, f32[4,4,64,1024]{3,2,1,0:T(8,128)}) custom-call(s32[4]{0:T(128)} %dates_hbm.3, s32[4,64]{1,0:T(4,128)} %keep_hbm.1, f32[4,64,1024]{2,1,0:T(8,128)} %re_hbm.3, f32[4,64,1024]{2,1,0:T(8,128)} %im_hbm.3, f32[4,8,1024]{2,1,0:T(8,128)S(1)} %get-tuple-element.8.left, f32[4,8,1024]{2,1,0:T(8,128)S(1)} %get-tuple-element.9.right, ...), custom_call_target="tpu_custom_call" | custom-call | tf_op jit(solution)/shard_map/coherence/pallas_call | solution.py:568

commit v4 on v3

--- a/solution.py
+++ b/solution.py
@@ -96,6 +96,8 @@
     right,
     b_ext,
     pow_b,
+    first_re,
+    first_im,
     dates_ref,
     offsets_ref,
     re_ref,
@@ -103,14 +105,19 @@
     band,
     prod,
     wide,
+    a_ext,
+    pow_a,
     load_sems,
+    first_edges,
     own_edges,
     packed,
     outward,
-    halves,
+    second_halves,
+    third_halves,
     first_half,
     merged,
-    pieces,
+    second_pieces,
+    third_pieces,
     pair_send,
     pair_recv,
     edge_send,
@@ -127,10 +134,14 @@
     rim_recv,
     rim_in_send,
     rim_in_recv,
+    top_send,
+    top_recv,
 ):
     me = lax.axis_index("date")
     tile = lax.axis_index("tile")
     chip, core = me // 2, me % 2
+    halves = (second_halves, third_halves)
+    pieces = (second_pieces, third_pieces)
     tiles = lax.axis_size("tile")
     next_tile = {"tile": lax.rem(tile + 1, tiles)}
     last_tile = {"tile": lax.rem(tile + tiles - 1, tiles)}
@@ -173,7 +184,7 @@
 
     for s in range(1, REFS):
         slot = lax.rem(dates_ref[s], DATE_DEV)
-        halves[core, s - 1, 0:4], halves[core, s - 1, 4:8] = half(slot, core)
+        halves[s - 1][core, 0:4], halves[s - 1][core, 4:8] = half(slot, core)
         outward[s - 1, 0:4], outward[s - 1, 4:8] = half(slot, 1 - core)
 
     @pl.when(me == 0)
@@ -189,9 +200,11 @@
 
     pl.semaphore_wait(barrier, 10)
 
-    to_sibling = remote(outward.at[pl.ds(0, 2)], halves.at[core], pair_send.at[0], pair_recv.at[0], sibling)
-    first_to_sibling = remote(outward.at[REFS - 1], first_half, pair_send.at[1], pair_recv.at[1], sibling)
-    to_sibling.start()
+    def to_sibling(n):
+        return remote(outward.at[n], halves[n].at[core], pair_send.at[n], pair_recv.at[n], sibling)
+
+    first_to_sibling = remote(outward.at[REFS - 1], first_half, pair_send.at[2], pair_recv.at[2], sibling)
+    to_sibling(0).start()
 
     def first_out(k):
         return remote(first_half.at[k], refs.at[0, core, k], first_send.at[k], first_recv.at[0], same_core(k))
@@ -210,31 +223,34 @@
 
     to_right = remote(own_edges, left, edge_send.at[0], edge_recv.at[0], next_tile)
     to_left = remote(own_edges, right, edge_send.at[1], edge_recv.at[1], last_tile)
+    to_sibling(1).start()
     to_right.start()
     to_left.start()
 
-    to_sibling.wait_recv()
-    for s in range(1, REFS):
-        owner_core = lax.rem(dates_ref[s] // DATE_DEV, 2)
-        merged[:, s - 1] = halves[owner_core, s - 1]
-
-    def gather(k):
-        return remote(merged.at[k], pieces.at[chip], gather_send.at[k], gather_recv.at[chip], same_core(k))
-
-    def gathered(k):
-        return remote(merged.at[k], pieces.at[k], gather_send.at[k], gather_recv.at[k], same_core(k))
-
-    @pl.loop(1, CHIPS)
-    def _(i):
-        gather(other(i)).start()
+    def gather(n, k):
+        return remote(merged.at[n, k], pieces[n].at[chip], gather_send.at[n, k], gather_recv.at[n, chip], same_core(k))
+
+    def gathered(n, k):
+        return remote(merged.at[n, k], pieces[n].at[k], gather_send.at[n, k], gather_recv.at[n, k], same_core(k))
 
     @pl.when(me == 1)
     def _():
         first_to_sibling.wait_recv()
         first_all()
 
+    for n in range(2):
+        to_sibling(n).wait_recv()
+        owner_core = lax.rem(dates_ref[n + 1] // DATE_DEV, 2)
+        merged[n] = halves[n][owner_core]
+
+        @pl.loop(1, CHIPS)
+        def _(i):
+            gather(n, other(i)).start()
+
+        pieces[n][chip] = merged[n, chip]
+
     def part(n, k):
-        return refs.at[0, core, k] if n == 0 else refs.at[pl.ds(1, 2), core, k]
+        return refs.at[n, core, k]
 
     def spread_out(n, k):
         return remote(part(n, chip), part(n, chip), spread_send.at[n, k], spread_recv.at[n, chip], same_core(k))
@@ -246,7 +262,7 @@
         return remote(part(n, k), part(n, k), inward_send.at[n, k], inward_recv.at[n, k], sibling)
 
     def inward_in(n, k):
-        there = refs.at[0, 1 - core, k] if n == 0 else refs.at[pl.ds(1, 2), 1 - core, k]
+        there = refs.at[n, 1 - core, k]
         return remote(there, there, inward_send.at[n, k], inward_recv.at[n, k], sibling)
 
     def spread_all(n):
@@ -261,12 +277,102 @@
         first_out(chip).wait_recv()
 
     spread_all(0)
-    pieces[chip] = merged[chip]
 
     to_right.wait()
     to_left.wait()
     has_top = (tile > 0).astype(jnp.float32)
     has_bottom = (tile < tiles - 1).astype(jnp.float32)
+
+    def first_edges_out(k, to):
+        return remote(first_edges, first_edges, top_send.at[k], top_recv.at[0], to)
+
+    @pl.when(me == 0)
+    def _():
+        first_edges[0:2] = left[0, 2:4]
+        first_edges[2:4] = left[0, 6:8]
+        first_edges[4:6] = right[0, 0:2]
+        first_edges[6:8] = right[0, 4:6]
+
+        @pl.loop(1, CHIPS)
+        def _(k):
+            first_edges_out(k, same_core(k)).start()
+
+        first_edges_out(0, sibling).start()
+
+    def take(n):
+        @pl.loop(1, CHIPS)
+        def _(i):
+            gathered(n, other(i)).wait_recv()
+
+        refs[n + 1, core, chip] = pieces[n][dates_ref[n + 1] // (2 * DATE_DEV)]
+
+    take(0)
+    spread_all(1)
+    take(1)
+
+    below = (core == 0) & (lax.rem(chip, 4) == 0)
+    above = (core == 1) & (lax.rem(chip, 4) == 3)
+    own_kind = jnp.where(core == 0, 0, 2) + chip // 4
+
+    def rim_over(to):
+        return remote(packed, ref_edges.at[own_kind], rim_send.at[0], rim_recv.at[4], to)
+
+    @pl.when(below)
+    def _():
+        for s in range(REFS):
+            packed[2 * s : 2 * s + 2] = refs[s, core, chip, 0:2]
+        packed[6:8] = jnp.zeros((2, COLS), jnp.float32)
+        rim_over(last_tile).start()
+
+    @pl.when(above)
+    def _():
+        for s in range(REFS):
+            packed[2 * s : 2 * s + 2] = refs[s, core, chip, 6:8]
+        packed[6:8] = jnp.zeros((2, COLS), jnp.float32)
+        rim_over(next_tile).start()
+
+    spread_all(2)
+
+    def rim_out(k):
+        return remote(ref_edges.at[own_kind], ref_edges.at[own_kind], rim_send.at[1 + k], rim_recv.at[own_kind], same_core(k))
+
+    def rim_in(kind):
+        return remote(ref_edges.at[kind], ref_edges.at[kind], rim_send.at[0], rim_recv.at[kind], sibling)
+
+    def rim_inward(kind):
+        return remote(ref_edges.at[kind], ref_edges.at[kind], rim_in_send.at[kind], rim_in_recv.at[kind], sibling)
+
+    def pass_on(n):
+        @pl.loop(1, CHIPS)
+        def _(i):
+            k = other(i)
+            spread_in(n, k).wait_recv()
+            inward(n, k).start()
+
+    def passed_on(n):
+        @pl.loop(0, CHIPS)
+        def _(k):
+            inward_in(n, k).wait_recv()
+
+    @pl.when(me > 0)
+    def _():
+        first_edges_out(0, sibling).wait_recv()
+
+    @pl.when((me > 0) & (core == 0))
+    def _():
+        first_edges_out(0, sibling).start()
+
+    @pl.when(below | above)
+    def _():
+        rim_over(next_tile).wait_recv()
+
+        @pl.loop(1, CHIPS)
+        def _(i):
+            rim_out(other(i)).start()
+
+        rim_inward(own_kind).start()
+
+    pass_on(0)
 
     @pl.loop(0, DATE_DEV)
     def _(j):
@@ -284,62 +390,19 @@
         lay(b_ext.at[j], 1, shifted(im_ref[j]), above_rows[6:8], below_rows[4:6])
         power(b_ext.at[j], pow_b.at[j], prod, wide, band)
 
-    @pl.loop(1, CHIPS)
-    def _(i):
-        gathered(other(i)).wait_recv()
-
-    for s in range(1, REFS):
-        refs[s, core, chip] = pieces[dates_ref[s] // (2 * DATE_DEV), s - 1]
-
-    below = (core == 0) & (lax.rem(chip, 4) == 0)
-    above = (core == 1) & (lax.rem(chip, 4) == 3)
-    own_kind = jnp.where(core == 0, 0, 2) + chip // 4
-
-    def rim_over(to):
-        return remote(packed, ref_edges.at[own_kind], rim_send.at[0], rim_recv.at[4], to)
-
-    @pl.when(below)
-    def _():
-        for s in range(REFS):
-            packed[2 * s : 2 * s + 2] = refs[s, core, chip, 0:2]
-        packed[6:8] = jnp.zeros((2, COLS), jnp.float32)
-        rim_over(last_tile).start()
-
-    @pl.when(above)
-    def _():
-        for s in range(REFS):
-            packed[2 * s : 2 * s + 2] = refs[s, core, chip, 6:8]
-        packed[6:8] = jnp.zeros((2, COLS), jnp.float32)
-        rim_over(next_tile).start()
-
-    spread_all(1)
-
-    def rim_out(k):
-        return remote(ref_edges.at[own_kind], ref_edges.at[own_kind], rim_send.at[1 + k], rim_recv.at[own_kind], same_core(k))
-
-    def rim_in(kind):
-        return remote(ref_edges.at[kind], ref_edges.at[kind], rim_send.at[0], rim_recv.at[kind], sibling)
-
-    def rim_inward(kind):
-        return remote(ref_edges.at[kind], ref_edges.at[kind], rim_in_send.at[kind], rim_in_recv.at[kind], sibling)
-
-    @pl.when(below | above)
-    def _():
-        rim_over(next_tile).wait_recv()
-
-        @pl.loop(1, CHIPS)
-        def _(i):
-            rim_out(other(i)).start()
-
-        rim_inward(own_kind).start()
-
-    for n in range(2):
-
-        @pl.loop(1, CHIPS)
-        def _(i):
-            k = other(i)
-            spread_in(n, k).wait_recv()
-            inward(n, k).start()
+    passed_on(0)
+    for p in range(2):
+        rows = refs[0, :, 4 * p : 4 * p + 4].reshape(ROWS, COLS)
+        top = first_edges[2 * p : 2 * p + 2] * has_top
+        bottom = first_edges[2 * p + 4 : 2 * p + 6] * has_bottom
+        lay(a_ext, p, rows, top, bottom)
+    power(a_ext, pow_a, prod, wide, band)
+
+    @pl.loop(0, DATE_DEV)
+    def _(j):
+        coherence(a_ext, pow_a, b_ext.at[j], pow_b.at[j], first_re.at[j], first_im.at[j], prod, wide, band)
+
+    pass_on(1)
 
     @pl.loop(0, 2)
     def _(m):
@@ -350,22 +413,29 @@
             rim_in(kind).wait_recv()
             rim_inward(kind).start()
 
-    for n in range(2):
-
-        @pl.loop(0, CHIPS)
-        def _(k):
-            inward_in(n, k).wait_recv()
+    pass_on(2)
+    passed_on(1)
+    passed_on(2)
 
     @pl.loop(0, 2)
     def _(m):
         rim_inward((1 - core) * 2 + m).wait_recv()
         rim_inward(core * 2 + m).wait_send()
 
-    to_sibling.wait_send()
+    to_sibling(0).wait_send()
+    to_sibling(1).wait_send()
+
+    @pl.when(core == 0)
+    def _():
+        first_edges_out(0, sibling).wait_send()
 
     @pl.when(me == 0)
     def _():
         first_to_sibling.wait_send()
+
+        @pl.loop(1, CHIPS)
+        def _(k):
+            first_edges_out(k, same_core(k)).wait_send()
 
     @pl.when(chip == 0)
     def _():
@@ -381,11 +451,13 @@
         def _(i):
             rim_out(other(i)).wait_send()
 
-    @pl.loop(1, CHIPS)
-    def _(i):
-        gather(other(i)).wait_send()
-
     for n in range(2):
+
+        @pl.loop(1, CHIPS)
+        def _(i):
+            gather(n, other(i)).wait_send()
+
+    for n in range(REFS):
 
         @pl.loop(1, CHIPS)
         def _(i):
@@ -410,9 +482,11 @@
             jax.ShapeDtypeStruct((DATE_DEV, 8, COLS), f32),
             jax.ShapeDtypeStruct((DATE_DEV, 2, BLOCKS, 72, 128), f32),
             jax.ShapeDtypeStruct((DATE_DEV, BLOCKS, ROWS, 128), f32),
+            jax.ShapeDtypeStruct((DATE_DEV, ROWS, COLS), f32),
+            jax.ShapeDtypeStruct((DATE_DEV, ROWS, COLS), f32),
         ),
         in_specs=[hbm] * 4,
-        out_specs=(vmem,) * 6,
+        out_specs=(vmem,) * 8,
         scratch_shapes=[
             pltpu.SMEM((STEPS,), jnp.int32),
             pltpu.SMEM((dates_all,), jnp.int32),
@@ -421,30 +495,37 @@
             pltpu.VMEM((256, 256), jnp.bfloat16),
             pltpu.VMEM((2, BLOCKS, 72, 128), f32),
             pltpu.VMEM((BLOCKS, 2 * ROWS, 256), jnp.bfloat16),
+            pltpu.VMEM((2, BLOCKS, 72, 128), f32),
+            pltpu.VMEM((BLOCKS, ROWS, 128), f32),
             dma((4,)),
+            pltpu.VMEM((8, COLS), f32),
             pltpu.VMEM((DATE_DEV, 8, COLS), f32),
             pltpu.VMEM((8, COLS), f32),
             pltpu.VMEM((REFS, CHIPS, 8, COLS), f32),
-            pltpu.VMEM((2, 2, CHIPS, 8, COLS), f32),
+            pltpu.VMEM((2, CHIPS, 8, COLS), f32),
+            pltpu.VMEM((2, CHIPS, 8, COLS), f32),
             pltpu.VMEM((CHIPS, 8, COLS), f32),
-            pltpu.VMEM((CHIPS, 2, 8, COLS), f32),
-            pltpu.VMEM((CHIPS, 2, 8, COLS), f32),
-            dma((2,)),
-            dma((2,)),
+            pltpu.VMEM((2, CHIPS, 8, COLS), f32),
+            pltpu.VMEM((CHIPS, 8, COLS), f32),
+            pltpu.VMEM((CHIPS, 8, COLS), f32),
+            dma((3,)),
+            dma((3,)),
             dma((2,)),
             dma((2,)),
             dma((CHIPS,)),
             dma((1,)),
-            dma((CHIPS,)),
-            dma((CHIPS,)),
             dma((2, CHIPS)),
             dma((2, CHIPS)),
-            dma((2, CHIPS)),
-            dma((2, CHIPS)),
+            dma((REFS, CHIPS)),
+            dma((REFS, CHIPS)),
+            dma((REFS, CHIPS)),
+            dma((REFS, CHIPS)),
             dma((CHIPS + 1,)),
             dma((5,)),
             dma((4,)),
             dma((4,)),
+            dma((CHIPS,)),
+            dma((1,)),
         ],
         compiler_params=pltpu.CompilerParams(collective_id=0, has_side_effects=True, vmem_limit_bytes=VMEM_LIMIT),
         name="spread",
@@ -462,6 +543,8 @@
     ref_edges,
     b_ext,
     pow_b,
+    first_re,
+    first_im,
     out_re,
     out_im,
     dates_ref,
@@ -487,7 +570,13 @@
         return pltpu.make_async_copy(zeros, outs[p].at[s, j], out_sems.at[p, s, j])
 
     def value_out(s, j, p):
-        return pltpu.make_async_copy(stage.at[p, s, j], outs[p].at[s, j], out_sems.at[p, s, j])
+        return pltpu.make_async_copy(stage.at[p, s - 1, j], outs[p].at[s, j], out_sems.at[p, s, j])
+
+    def first_out(j, p):
+        return pltpu.make_async_copy((first_re, first_im)[p].at[j], outs[p].at[0, j], out_sems.at[p, 0, j])
+
+    slot = DATE_DEV - 2
+    own_loads = [pltpu.make_async_copy(h.at[slot], own.at[p], own_sems.at[p]) for p, h in enumerate((re_hbm, im_hbm))]
 
     def valid(s, j):
         date = me * DATE_DEV + j
@@ -511,10 +600,24 @@
                 zero_out(s, j, 0).start()
                 zero_out(s, j, 1).start()
 
+    @pl.loop(0, DATE_DEV)
+    def _(j):
+        @pl.when(valid(0, j))
+        def _():
+            first_out(j, 0).start()
+            first_out(j, 1).start()
+
+    last = valid(REFS, DATE_DEV - 1)
+
+    @pl.when(last)
+    def _():
+        for c in own_loads:
+            c.start()
+
     def edge_rows(tile_rows, at):
         return jnp.where(at == 0, tile_rows[0:2], jnp.where(at == 1, tile_rows[2:4], tile_rows[4:6]))
 
-    @pl.loop(0, STEPS)
+    @pl.loop(1, STEPS)
     def _(s):
         some = valid(s, 0) | valid(s, 1) | valid(s, 2) | valid(s, 3)
 
@@ -529,11 +632,7 @@
 
         @pl.when(some & (s == REFS))
         def _():
-            slot = DATE_DEV - 2
-            loads = [pltpu.make_async_copy(h.at[slot], own.at[p], own_sems.at[p]) for p, h in enumerate((re_hbm, im_hbm))]
-            for c in loads:
-                c.start()
-            for c in loads:
+            for c in own_loads:
                 c.wait()
             for p in range(2):
                 top = left[slot, 4 * p + 2 : 4 * p + 4] * has_top
@@ -548,7 +647,7 @@
         def _(j):
             @pl.when(valid(s, j))
             def _():
-                coherence(a_ext, pow_a, b_ext.at[j], pow_b.at[j], stage.at[0, s, j], stage.at[1, s, j], prod, wide, band)
+                coherence(a_ext, pow_a, b_ext.at[j], pow_b.at[j], stage.at[0, s - 1, j], stage.at[1, s - 1, j], prod, wide, band)
                 value_out(s, j, 0).start()
                 value_out(s, j, 1).start()
 
@@ -556,11 +655,11 @@
     def _(s):
         @pl.loop(0, DATE_DEV)
         def _(j):
-            value_out(s, j, 0).wait()
-            value_out(s, j, 1).wait()
-
-
-def compute(dates, keep, slc_re, slc_im, left, right, refs, ref_edges, b_ext, pow_b):
+            zero_out(s, j, 0).wait()
+            zero_out(s, j, 1).wait()
+
+
+def compute(dates, keep, slc_re, slc_im, *parts):
     vmem = pl.BlockSpec(memory_space=pltpu.VMEM)
     hbm = pl.BlockSpec(memory_space=pltpu.HBM)
     shape = jax.ShapeDtypeStruct((STEPS, DATE_DEV, ROWS, COLS), jnp.float32)
@@ -568,7 +667,7 @@
     return pl.pallas_call(
         compute_kernel,
         out_shape=(shape, shape),
-        in_specs=[hbm] * 4 + [vmem] * 6,
+        in_specs=[hbm] * 4 + [vmem] * len(parts),
         out_specs=(hbm, hbm),
         scratch_shapes=[
             pltpu.SMEM((STEPS,), jnp.int32),
@@ -576,7 +675,7 @@
             pltpu.VMEM((256, 256), jnp.bfloat16),
             pltpu.VMEM((2, ROWS, COLS), f32),
             pltpu.VMEM((ROWS, COLS), f32),
-            pltpu.VMEM((2, STEPS, DATE_DEV, ROWS, COLS), f32),
+            pltpu.VMEM((2, REFS, DATE_DEV, ROWS, COLS), f32),
             pltpu.VMEM((2, BLOCKS, 72, 128), f32),
             pltpu.VMEM((2, BLOCKS, 72, 128), f32),
             pltpu.VMEM((BLOCKS, 2 * ROWS, 256), jnp.bfloat16),
@@ -586,14 +685,15 @@
         ],
         compiler_params=pltpu.CompilerParams(vmem_limit_bytes=VMEM_LIMIT),
         name="coherence",
-    )(dates, keep, slc_re, slc_im, left, right, refs, ref_edges, b_ext, pow_b)
+    )(dates, keep, slc_re, slc_im, *parts)
 
 
 def body(slc_re, slc_im, ref_dates, pair_keep, col_offsets):
     hbm = [pltpu.with_memory_space_constraint(x, pltpu.HBM) for x in (slc_re, slc_im, ref_dates, pair_keep, col_offsets)]
     slc_re, slc_im, ref_dates, pair_keep, col_offsets = hbm
-    refs, ref_edges, left, right, b_ext, pow_b = spread(ref_dates, col_offsets, slc_re, slc_im)
-    return compute(ref_dates, pair_keep, slc_re, slc_im, left, right, refs, ref_edges, b_ext, pow_b)
+    parts = spread(ref_dates, col_offsets, slc_re, slc_im)
+    order = (2, 3, 0, 1, 4, 5, 6, 7)
+    return compute(ref_dates, pair_keep, slc_re, slc_im, *[parts[k] for k in order])
 
 
 def solution(mesh):

time: 42.5 us -> 41.3 us (0.972)
  Pallas kernels: 41.3 us -> 40.2 us
    pallas_call x1, Pallas kernels: 36.9 us -> 35.8 us  [spread(): pl.pallas_call(spread_kernel, out_shape=(jax.ShapeDtypeStruct((REFS, 2, C...]
where the time goes in v4:
time: 41.3 us; the launch traced here: 40.8 us
  Pallas kernels  40.2 us (97%)
  between operations  0.64 us (2%)
    pallas_call x1, Pallas kernels, spread(): pl.pallas_call(spread_kernel, out_shape=(jax.ShapeDtypeStruct((REFS, 2, C...  35.8 us
    pallas_call x1, Pallas kernels, compute(): pl.pallas_call(compute_kernel, out_shape=(shape, shape), in_specs=[hbm] *...  4.36 us

profile of v4, /device:TPU:1, one launch (start us, length us, event | category | flops | bytes accessed | tf_op | source)
XLA Modules:
  0.0 40.8 jit_solution(3963845653099620543)
XLA Ops:
  0.6 35.8 %spread.1 = (f32[3,2,8,8,1024]{4,3,2,1,0:T(8,128)S(1)}, f32[4,8,1024]{2,1,0:T(8,128)S(1)}, f32[4,8,1024]{2,1,0:T(8,128)S(1)}, f32[4,8,1024]{2,1,0:T(8,128)S(1)},...) custom-call(s32[4]{0:T(128)} %dates_hbm.3, ...), custom_call_target="tpu_custom_call" | custom-call | tf_op jit(solution)/shard_map/spread/pallas_call | solution.py:476
  36.4 4.4 %coherence.1 = (f32[4,4,64,1024]{3,2,1,0:T(8,128)}, f32[4,4,64,1024]{3,2,1,0:T(8,128)}) custom-call(s32[4]{0:T(128)} %dates_hbm.3, s32[4,64]{1,0:T(4,128)} %keep_hbm.1, f32[4,64,1024]{2,1,0:T(8,128)} %re_hbm.3, f32[4,64,1024]{2,1,0:T(8,128)} %im_hbm.3, f32[4,8,1024]{2,1,0:T(8,128)S(1)} %get-tuple-element.10.left, f32[4,8,1024]{2,1,0:T(8,128)S(1)} %get-tuple-element.11.right, ...), custom_call_target="tpu_custom_call" | custom-call | tf_op jit(solution)/shard_map/coherence/pallas_call | solution.py:667

commit v5 on v4

--- a/solution.py
+++ b/solution.py
@@ -109,7 +109,8 @@
     pow_a,
     load_sems,
     first_edges,
-    own_edges,
+    edges_right,
+    edges_left,
     packed,
     outward,
     second_halves,
@@ -193,10 +194,10 @@
         outward[REFS - 1, 0:4], outward[REFS - 1, 4:8] = half(0, 1)
 
     for j in range(DATE_DEV):
-        own_edges[j, 0:2] = re_ref[j, 0:2]
-        own_edges[j, 2:4] = re_ref[j, ROWS - 2 : ROWS]
-        own_edges[j, 4:6] = im_ref[j, 0:2]
-        own_edges[j, 6:8] = im_ref[j, ROWS - 2 : ROWS]
+        at = 4 * (j % 2)
+        for p, plane in enumerate((re_ref, im_ref)):
+            edges_right[j // 2, at + 2 * p : at + 2 * p + 2] = plane[j, ROWS - 2 : ROWS]
+            edges_left[j // 2, at + 2 * p : at + 2 * p + 2] = plane[j, 0:2]
 
     pl.semaphore_wait(barrier, 10)
 
@@ -205,6 +206,10 @@
 
     first_to_sibling = remote(outward.at[REFS - 1], first_half, pair_send.at[2], pair_recv.at[2], sibling)
     to_sibling(0).start()
+    to_right = remote(edges_right, left, edge_send.at[0], edge_recv.at[0], next_tile)
+    to_left = remote(edges_left, right, edge_send.at[1], edge_recv.at[1], last_tile)
+    to_right.start()
+    to_left.start()
 
     def first_out(k):
         return remote(first_half.at[k], refs.at[0, core, k], first_send.at[k], first_recv.at[0], same_core(k))
@@ -221,11 +226,7 @@
         first_to_sibling.start()
         first_all()
 
-    to_right = remote(own_edges, left, edge_send.at[0], edge_recv.at[0], next_tile)
-    to_left = remote(own_edges, right, edge_send.at[1], edge_recv.at[1], last_tile)
     to_sibling(1).start()
-    to_right.start()
-    to_left.start()
 
     def gather(n, k):
         return remote(merged.at[n, k], pieces[n].at[chip], gather_send.at[n, k], gather_recv.at[n, chip], same_core(k))
@@ -288,10 +289,8 @@
 
     @pl.when(me == 0)
     def _():
-        first_edges[0:2] = left[0, 2:4]
-        first_edges[2:4] = left[0, 6:8]
-        first_edges[4:6] = right[0, 0:2]
-        first_edges[6:8] = right[0, 4:6]
+        first_edges[0:4] = left[0, 0:4]
+        first_edges[4:8] = right[0, 0:4]
 
         @pl.loop(1, CHIPS)
         def _(k):
@@ -384,10 +383,14 @@
             column = lax.broadcasted_iota(jnp.int32, x.shape, 1)
             return jnp.where(column < COLS - offset, x, 0.0)
 
-        above_rows = shifted(left[j]) * has_top
-        below_rows = shifted(right[j]) * has_bottom
-        lay(b_ext.at[j], 0, shifted(re_ref[j]), above_rows[2:4], below_rows[0:2])
-        lay(b_ext.at[j], 1, shifted(im_ref[j]), above_rows[6:8], below_rows[4:6])
+        def edges_of(side):
+            both = side[j // 2]
+            return jnp.where(lax.rem(j, 2) == 0, both[0:4], both[4:8])
+
+        above_rows = shifted(edges_of(left)) * has_top
+        below_rows = shifted(edges_of(right)) * has_bottom
+        lay(b_ext.at[j], 0, shifted(re_ref[j]), above_rows[0:2], below_rows[0:2])
+        lay(b_ext.at[j], 1, shifted(im_ref[j]), above_rows[2:4], below_rows[2:4])
         power(b_ext.at[j], pow_b.at[j], prod, wide, band)
 
     passed_on(0)
@@ -478,8 +481,8 @@
         out_shape=(
             jax.ShapeDtypeStruct((REFS, 2, CHIPS, 8, COLS), f32),
             jax.ShapeDtypeStruct((4, 8, COLS), f32),
-            jax.ShapeDtypeStruct((DATE_DEV, 8, COLS), f32),
-            jax.ShapeDtypeStruct((DATE_DEV, 8, COLS), f32),
+            jax.ShapeDtypeStruct((2, 8, COLS), f32),
+            jax.ShapeDtypeStruct((2, 8, COLS), f32),
             jax.ShapeDtypeStruct((DATE_DEV, 2, BLOCKS, 72, 128), f32),
             jax.ShapeDtypeStruct((DATE_DEV, BLOCKS, ROWS, 128), f32),
             jax.ShapeDtypeStruct((DATE_DEV, ROWS, COLS), f32),
@@ -499,7 +502,8 @@
             pltpu.VMEM((BLOCKS, ROWS, 128), f32),
             dma((4,)),
             pltpu.VMEM((8, COLS), f32),
-            pltpu.VMEM((DATE_DEV, 8, COLS), f32),
+            pltpu.VMEM((2, 8, COLS), f32),
+            pltpu.VMEM((2, 8, COLS), f32),
             pltpu.VMEM((8, COLS), f32),
             pltpu.VMEM((REFS, CHIPS, 8, COLS), f32),
             pltpu.VMEM((2, CHIPS, 8, COLS), f32),
@@ -635,8 +639,8 @@
             for c in own_loads:
                 c.wait()
             for p in range(2):
-                top = left[slot, 4 * p + 2 : 4 * p + 4] * has_top
-                bottom = right[slot, 4 * p : 4 * p + 2] * has_bottom
+                top = left[slot // 2, 2 * p : 2 * p + 2] * has_top
+                bottom = right[slot // 2, 2 * p : 2 * p + 2] * has_bottom
                 lay(a_ext, p, own[p], top, bottom)
 
         @pl.when(some)

time: 41.3 us -> 39.9 us (0.966)
  Pallas kernels: 40.2 us -> 38.8 us
    pallas_call x1, Pallas kernels: 35.8 us -> 34.4 us  [spread(): pl.pallas_call(spread_kernel, out_shape=(jax.ShapeDtypeStruct((REFS, 2, C...]
where the time goes in v5:
time: 39.9 us; the launch traced here: 39.5 us
  Pallas kernels  38.8 us (97%)
  between operations  0.64 us (2%)
    pallas_call x1, Pallas kernels, spread(): pl.pallas_call(spread_kernel, out_shape=(jax.ShapeDtypeStruct((REFS, 2, C...  34.4 us
    pallas_call x1, Pallas kernels, compute(): pl.pallas_call(compute_kernel, out_shape=(shape, shape), in_specs=[hbm] *...  4.42 us

profile of v5, /device:TPU:1, one launch (start us, length us, event | category | flops | bytes accessed | tf_op | source)
XLA Modules:
  0.0 39.5 jit_solution(9442912108137047813)
XLA Ops:
  0.6 34.4 %spread.1 = (f32[3,2,8,8,1024]{4,3,2,1,0:T(8,128)S(1)}, f32[4,8,1024]{2,1,0:T(8,128)S(1)}, f32[2,8,1024]{2,1,0:T(8,128)S(1)}, f32[2,8,1024]{2,1,0:T(8,128)S(1)},...) custom-call(s32[4]{0:T(128)} %dates_hbm.3, ...), custom_call_target="tpu_custom_call" | custom-call | tf_op jit(solution)/shard_map/spread/pallas_call | solution.py:479
  35.0 4.4 %coherence.1 = (f32[4,4,64,1024]{3,2,1,0:T(8,128)}, f32[4,4,64,1024]{3,2,1,0:T(8,128)}) custom-call(s32[4]{0:T(128)} %dates_hbm.3, s32[4,64]{1,0:T(4,128)} %keep_hbm.1, f32[4,64,1024]{2,1,0:T(8,128)} %re_hbm.3, f32[4,64,1024]{2,1,0:T(8,128)} %im_hbm.3, f32[2,8,1024]{2,1,0:T(8,128)S(1)} %get-tuple-element.10.left, f32[2,8,1024]{2,1,0:T(8,128)S(1)} %get-tuple-element.11.right, ...), custom_call_target="tpu_custom_call" | custom-call | tf_op jit(solution)/shard_map/coherence/pallas_call | solution.py:671

commit v6 on v5

--- a/solution.py
+++ b/solution.py
@@ -330,8 +330,6 @@
         packed[6:8] = jnp.zeros((2, COLS), jnp.float32)
         rim_over(next_tile).start()
 
-    spread_all(2)
-
     def rim_out(k):
         return remote(ref_edges.at[own_kind], ref_edges.at[own_kind], rim_send.at[1 + k], rim_recv.at[own_kind], same_core(k))
 
@@ -340,6 +338,18 @@
 
     def rim_inward(kind):
         return remote(ref_edges.at[kind], ref_edges.at[kind], rim_in_send.at[kind], rim_in_recv.at[kind], sibling)
+
+    @pl.when(below | above)
+    def _():
+        rim_over(next_tile).wait_recv()
+
+        @pl.loop(1, CHIPS)
+        def _(i):
+            rim_out(other(i)).start()
+
+        rim_inward(own_kind).start()
+
+    spread_all(2)
 
     def pass_on(n):
         @pl.loop(1, CHIPS)
@@ -360,16 +370,6 @@
     @pl.when((me > 0) & (core == 0))
     def _():
         first_edges_out(0, sibling).start()
-
-    @pl.when(below | above)
-    def _():
-        rim_over(next_tile).wait_recv()
-
-        @pl.loop(1, CHIPS)
-        def _(i):
-            rim_out(other(i)).start()
-
-        rim_inward(own_kind).start()
 
     pass_on(0)
 
@@ -582,15 +582,26 @@
     slot = DATE_DEV - 2
     own_loads = [pltpu.make_async_copy(h.at[slot], own.at[p], own_sems.at[p]) for p, h in enumerate((re_hbm, im_hbm))]
 
+    def past_last(j):
+        return me * DATE_DEV + j == lax.axis_size("date") * DATE_DEV - 1
+
     def valid(s, j):
         date = me * DATE_DEV + j
-        return (keep_ref[s, date] == 1) & (date > dates_ref[s])
+        return (keep_ref[s, date] == 1) & (date > dates_ref[s]) & ((s < REFS) | past_last(j))
 
     scalars = ((dates_hbm, dates_ref), (keep_hbm, keep_ref))
     loads = [pltpu.make_async_copy(a, b, own_sems.at[2 + k]) for k, (a, b) in enumerate(scalars)]
     for c in loads:
         c.start()
     zeros[...] = jnp.zeros_like(zeros)
+
+    @pl.loop(0, DATE_DEV)
+    def _(j):
+        @pl.when(jnp.logical_not(past_last(j)))
+        def _():
+            zero_out(REFS, j, 0).start()
+            zero_out(REFS, j, 1).start()
+
     band[...] = band_matrix()
     for c in loads:
         c.wait()
@@ -599,7 +610,7 @@
     def _(s):
         @pl.loop(0, DATE_DEV)
         def _(j):
-            @pl.when(jnp.logical_not(valid(s, j)))
+            @pl.when(jnp.logical_not(valid(s, j)) & ((s < REFS) | past_last(j)))
             def _():
                 zero_out(s, j, 0).start()
                 zero_out(s, j, 1).start()

time: 39.9 us -> 39.6 us (level)
  the two profiles are of different devices: /device:TPU:1 before, /device:TPU:121 now
where the time goes in v6:
time: 39.6 us; the launch traced here: 40.1 us
  Pallas kernels  39.5 us (100%)
  between operations  0.64 us (2%)
    pallas_call x1, Pallas kernels, spread(): pl.pallas_call(spread_kernel, out_shape=(jax.ShapeDtypeStruct((REFS, 2, C...  32.2 us
    pallas_call x1, Pallas kernels, compute(): pl.pallas_call(compute_kernel, out_shape=(shape, shape), in_specs=[hbm] *...  7.31 us

profile of v6, /device:TPU:121, one launch (start us, length us, event | category | flops | bytes accessed | tf_op | source)
XLA Modules:
  0.0 40.1 jit_solution(13539982810699620571)
XLA Ops:
  0.6 32.2 %spread.1 = (f32[3,2,8,8,1024]{4,3,2,1,0:T(8,128)S(1)}, f32[4,8,1024]{2,1,0:T(8,128)S(1)}, f32[2,8,1024]{2,1,0:T(8,128)S(1)}, f32[2,8,1024]{2,1,0:T(8,128)S(1)},...) custom-call(s32[4]{0:T(128)} %dates_hbm.3, ...), custom_call_target="tpu_custom_call" | custom-call | tf_op jit(solution)/shard_map/spread/pallas_call | solution.py:479
  32.8 7.3 %coherence.1 = (f32[4,4,64,1024]{3,2,1,0:T(8,128)}, f32[4,4,64,1024]{3,2,1,0:T(8,128)}) custom-call(s32[4]{0:T(128)} %dates_hbm.3, s32[4,64]{1,0:T(4,128)} %keep_hbm.1, f32[4,64,1024]{2,1,0:T(8,128)} %re_hbm.3, f32[4,64,1024]{2,1,0:T(8,128)} %im_hbm.3, f32[2,8,1024]{2,1,0:T(8,128)S(1)} %get-tuple-element.10.left, f32[2,8,1024]{2,1,0:T(8,128)S(1)} %get-tuple-element.11.right, ...), custom_call_target="tpu_custom_call" | custom-call | tf_op jit(solution)/shard_map/coherence/pallas_call | solution.py:682

commit v7 on v6

--- a/solution.py
+++ b/solution.py
@@ -602,7 +602,20 @@
             zero_out(REFS, j, 0).start()
             zero_out(REFS, j, 1).start()
 
+    def edge_rows(tile_rows, at):
+        return jnp.where(at == 0, tile_rows[0:2], jnp.where(at == 1, tile_rows[2:4], tile_rows[4:6]))
+
+    def lay_reference(at):
+        for p in range(2):
+            rows = refs[at, :, 4 * p : 4 * p + 4].reshape(ROWS, COLS)
+            top = edge_rows(ref_edges[2 + p], at) * has_top
+            bottom = edge_rows(ref_edges[p], at) * has_bottom
+            lay(a_ext, p, rows, top, bottom)
+
     band[...] = band_matrix()
+
+    lay_reference(1)
+    power(a_ext, pow_a, prod, wide, band)
     for c in loads:
         c.wait()
 
@@ -629,21 +642,13 @@
         for c in own_loads:
             c.start()
 
-    def edge_rows(tile_rows, at):
-        return jnp.where(at == 0, tile_rows[0:2], jnp.where(at == 1, tile_rows[2:4], tile_rows[4:6]))
-
     @pl.loop(1, STEPS)
     def _(s):
         some = valid(s, 0) | valid(s, 1) | valid(s, 2) | valid(s, 3)
 
-        @pl.when(some & (s < REFS))
+        @pl.when(some & (s > 1) & (s < REFS))
         def _():
-            at = jnp.minimum(s, REFS - 1)
-            for p in range(2):
-                rows = refs[at, :, 4 * p : 4 * p + 4].reshape(ROWS, COLS)
-                top = edge_rows(ref_edges[2 + p], at) * has_top
-                bottom = edge_rows(ref_edges[p], at) * has_bottom
-                lay(a_ext, p, rows, top, bottom)
+            lay_reference(REFS - 1)
 
         @pl.when(some & (s == REFS))
         def _():
@@ -654,7 +659,7 @@
                 bottom = right[slot // 2, 2 * p : 2 * p + 2] * has_bottom
                 lay(a_ext, p, own[p], top, bottom)
 
-        @pl.when(some)
+        @pl.when(some & (s > 1))
         def _():
             power(a_ext, pow_a, prod, wide, band)
 

time: 39.6 us -> 39.1 us (0.987)
  the two profiles are of different devices: /device:TPU:121 before, /device:TPU:1 now
where the time goes in v7:
time: 39.1 us; the launch traced here: 38.6 us
  Pallas kernels  37.9 us (97%)
  between operations  0.64 us (2%)
    pallas_call x1, Pallas kernels, spread(): pl.pallas_call(spread_kernel, out_shape=(jax.ShapeDtypeStruct((REFS, 2, C...  34.2 us
    pallas_call x1, Pallas kernels, compute(): pl.pallas_call(compute_kernel, out_shape=(shape, shape), in_specs=[hbm] *...  3.7 us

profile of v7, /device:TPU:1, one launch (start us, length us, event | category | flops | bytes accessed | tf_op | source)
XLA Modules:
  0.0 38.6 jit_solution(8011922209544718173)
XLA Ops:
  0.6 34.2 %spread.1 = (f32[3,2,8,8,1024]{4,3,2,1,0:T(8,128)S(1)}, f32[4,8,1024]{2,1,0:T(8,128)S(1)}, f32[2,8,1024]{2,1,0:T(8,128)S(1)}, f32[2,8,1024]{2,1,0:T(8,128)S(1)},...) custom-call(s32[4]{0:T(128)} %dates_hbm.3, ...), custom_call_target="tpu_custom_call" | custom-call | tf_op jit(solution)/shard_map/spread/pallas_call | solution.py:479
  34.9 3.7 %coherence.1 = (f32[4,4,64,1024]{3,2,1,0:T(8,128)}, f32[4,4,64,1024]{3,2,1,0:T(8,128)}) custom-call(s32[4]{0:T(128)} %dates_hbm.3, s32[4,64]{1,0:T(4,128)} %keep_hbm.1, f32[4,64,1024]{2,1,0:T(8,128)} %re_hbm.3, f32[4,64,1024]{2,1,0:T(8,128)} %im_hbm.3, f32[2,8,1024]{2,1,0:T(8,128)S(1)} %get-tuple-element.10.left, f32[2,8,1024]{2,1,0:T(8,128)S(1)} %get-tuple-element.11.right, ...), custom_call_target="tpu_custom_call" | custom-call | tf_op jit(solution)/shard_map/coherence/pallas_call | solution.py:687

commit v8 on v7

--- a/solution.py
+++ b/solution.py
@@ -154,6 +154,9 @@
     def other(i):
         return lax.rem(chip + i, CHIPS)
 
+    def sender(i):
+        return lax.rem(chip + CHIPS - i, CHIPS)
+
     def remote(source, target, send, recv, to):
         return pltpu.make_async_remote_copy(src_ref=source, dst_ref=target, send_sem=send, recv_sem=recv, device_id=to, device_id_type=MESH)
 
@@ -301,7 +304,7 @@
     def take(n):
         @pl.loop(1, CHIPS)
         def _(i):
-            gathered(n, other(i)).wait_recv()
+            gathered(n, sender(i)).wait_recv()
 
         refs[n + 1, core, chip] = pieces[n][dates_ref[n + 1] // (2 * DATE_DEV)]
 
@@ -354,7 +357,7 @@
     def pass_on(n):
         @pl.loop(1, CHIPS)
         def _(i):
-            k = other(i)
+            k = sender(i)
             spread_in(n, k).wait_recv()
             inward(n, k).start()
 

time: 39.1 us -> 39.2 us (level)
  no operation moved by 1% of the time
where the time goes in v8:
time: 39.2 us; the launch traced here: 38.8 us
  Pallas kernels  38.2 us (97%)
  between operations  0.64 us (2%)
    pallas_call x1, Pallas kernels, spread(): pl.pallas_call(spread_kernel, out_shape=(jax.ShapeDtypeStruct((REFS, 2, C...  34.5 us
    pallas_call x1, Pallas kernels, compute(): pl.pallas_call(compute_kernel, out_shape=(shape, shape), in_specs=[hbm] *...  3.72 us

profile of v8, /device:TPU:1, one launch (start us, length us, event | category | flops | bytes accessed | tf_op | source)
XLA Modules:
  0.0 38.8 jit_solution(13579391418601289923)
XLA Ops:
  0.6 34.5 %spread.1 = (f32[3,2,8,8,1024]{4,3,2,1,0:T(8,128)S(1)}, f32[4,8,1024]{2,1,0:T(8,128)S(1)}, f32[2,8,1024]{2,1,0:T(8,128)S(1)}, f32[2,8,1024]{2,1,0:T(8,128)S(1)},...) custom-call(s32[4]{0:T(128)} %dates_hbm.3, ...), custom_call_target="tpu_custom_call" | custom-call | tf_op jit(solution)/shard_map/spread/pallas_call | solution.py:482
  35.1 3.7 %coherence.1 = (f32[4,4,64,1024]{3,2,1,0:T(8,128)}, f32[4,4,64,1024]{3,2,1,0:T(8,128)}) custom-call(s32[4]{0:T(128)} %dates_hbm.3, s32[4,64]{1,0:T(4,128)} %keep_hbm.1, f32[4,64,1024]{2,1,0:T(8,128)} %re_hbm.3, f32[4,64,1024]{2,1,0:T(8,128)} %im_hbm.3, f32[2,8,1024]{2,1,0:T(8,128)S(1)} %get-tuple-element.10.left, f32[2,8,1024]{2,1,0:T(8,128)S(1)} %get-tuple-element.11.right, ...), custom_call_target="tpu_custom_call" | custom-call | tf_op jit(solution)/shard_map/coherence/pallas_call | solution.py:690
